TPU v7x, 32 devices: a whole 2x2x4 slice. The times are simulated.
32 devices in a mesh: pipe: 2 (over core), tensor: 4 (over z), dp: 4 (over y, x).
Axes of the slice: x: 2, y: 2, z: 4, core: 2. Of those that a mesh axis runs over, the one named last changes fastest.
Arguments:
- cotangent: bfloat16 [2, 2048, 8192], P(None, 'dp', 'tensor'), may hold values from -6 to 6
- saved_short: bfloat16 [2, 2, 2048, 8192], P('pipe', None, 'dp', 'tensor'), may hold values from -3.5 to 3.5
- saved_medium: bfloat16 [2, 2, 2048, 8192], P('pipe', None, 'dp', 'tensor'), may hold values from -3.5 to 3.5
- out_weight: bfloat16 [2, 8192, 8192], P('pipe', 'tensor'), may hold values from -0.0625 to 0.0625
- short_filter: float32 [2, 7, 8192], P('pipe', None, 'tensor'), may hold values from -2.5 to 2.5
- medium_filter: float32 [2, 128, 8192], P('pipe', None, 'tensor'), may hold values from -0.5 to 0.5
- proj_in: bfloat16 [2, 8192, 64], P('pipe', 'tensor'), may hold values from -0.0625 to 0.0625
- proj_out: bfloat16 [2, 8192, 64], P('pipe'), may hold values from -0.0625 to 0.0625
Outputs:
- proj_grads: float32 [2, 2, 64, 64], P('pipe')
All inputs are finite; a program needn't handle non-finite values.
Results may differ from a plain program's by a relative error of at most 0.0041.
Values may be sent and summed in bfloat16 or wider, within the bound.
A program may use at most 192 MiB of HBM per device.

v0:
```python
import math

import jax
import jax.numpy as jnp
from jax import lax
from jax.sharding import PartitionSpec as P


def passed_along(array, axis, by):
    devices = lax.axis_size(axis)
    pairs = [(i, i + by) for i in range(devices) if 0 <= i + by < devices]
    return lax.ppermute(array, axis, pairs)


def adjoint_filter(extended, filter_taps):
    return lax.conv_general_dilated(
        extended,
        filter_taps[:, None, :],
        (1,),
        "VALID",
        dimension_numbers=("NWC", "WIO", "NWC"),
        feature_group_count=extended.shape[2],
        precision=lax.Precision.HIGHEST,
    )


def layer_pass(
    gradient,
    short_low,
    medium_low,
    weight_rows,
    short_taps,
    medium_taps,
    in_basis,
    out_basis,
    norm_factor,
):
    micro_count, seq_dev, width_local = gradient.shape
    row_count = micro_count * seq_dev
    flat_grad = gradient.reshape(row_count, width_local)
    initial = (
        jnp.zeros((row_count, width_local), jnp.float32),
        jnp.zeros((row_count, out_basis.shape[1]), jnp.float32),
    )
    shard_piece = lax.all_gather(flat_grad, "tensor", axis=1, tiled=True)
    piece_width = shard_piece.shape[1]
    weight_cols = lax.slice_in_dim(weight_rows, 0, piece_width, axis=1)
    basis_rows = lax.slice_in_dim(out_basis, 0, piece_width, axis=0)
    back_part = lax.dot_general(
        shard_piece, weight_cols, (((1,), (1,)), ((), ())), preferred_element_type=jnp.float32
    )
    side_part = jnp.dot(shard_piece, basis_rows, preferred_element_type=jnp.float32)
    back_sum = initial[0] + back_part
    out_flat = initial[1] + side_part
    back_low = lax.optimization_barrier(back_sum.astype(jnp.bfloat16))
    back_grad = back_low.astype(jnp.float32).reshape(micro_count, seq_dev, width_local)
    short_act = short_low.astype(jnp.float32)
    medium_act = medium_low.astype(jnp.float32)
    gate_short = back_grad * medium_act
    gate_medium = back_grad * short_act
    rim_short, rim_medium = (
        passed_along(
            gate_short[:, : short_taps.shape[0] - 1].astype(jnp.bfloat16), "dp", -1
        ).astype(jnp.float32),
        passed_along(
            gate_medium[:, : medium_taps.shape[0] - 1].astype(jnp.bfloat16), "dp", -1
        ).astype(jnp.float32),
    )
    adj_short = adjoint_filter(jnp.concatenate([gate_short, rim_short], axis=1), short_taps)
    adj_medium = adjoint_filter(jnp.concatenate([gate_medium, rim_medium], axis=1), medium_taps)
    passed = (gradient.astype(jnp.float32) + adj_short + adj_medium).astype(jnp.bfloat16)
    gated = (short_act * medium_act).astype(jnp.bfloat16)
    in_part = jnp.dot(
        gated.reshape(row_count, width_local), in_basis, preferred_element_type=jnp.float32
    )
    out_side = out_flat.reshape(micro_count, seq_dev, -1)
    in_side = lax.psum(in_part, "tensor").reshape(micro_count, seq_dev, -1)
    local_grads = (
        jnp.einsum("mtr,mtq->mrq", in_side, out_side, precision=lax.Precision.HIGHEST) * norm_factor
    )
    layer_grads = lax.psum(local_grads, "dp")
    return (passed, layer_grads)


def body(
    cotangent, saved_short, saved_medium, out_weight, short_filter, medium_filter, proj_in, proj_out
):
    sections = lax.axis_size("pipe")
    section_index = lax.axis_index("pipe")
    is_top = section_index == sections - 1
    norm_factor = 1.0 / math.sqrt(cotangent.shape[1] * lax.axis_size("dp"))
    micro_count = cotangent.shape[0]
    rank_width = proj_in.shape[2]
    weight_rows = out_weight[0]
    short_taps = short_filter[0]
    medium_taps = medium_filter[0]
    in_basis = proj_in[0]
    out_basis = proj_out[0]
    kept_grads = jnp.zeros((micro_count, rank_width, rank_width), jnp.float32)
    received = jnp.zeros_like(cotangent)
    for section_turn in range(sections):
        incoming = jnp.where(is_top, cotangent, received)
        passed, layer_grads = layer_pass(
            incoming,
            saved_short[0],
            saved_medium[0],
            weight_rows,
            short_taps,
            medium_taps,
            in_basis,
            out_basis,
            norm_factor,
        )
        kept_grads = jnp.where(
            section_turn == sections - 1 - section_index, layer_grads, kept_grads
        )
        if section_turn < sections - 1:
            received = passed_along(passed, "pipe", -1)
    return kept_grads[None]


def solution(mesh):
    in_specs = (
        P(None, "dp", "tensor"),
        P("pipe", None, "dp", "tensor"),
        P("pipe", None, "dp", "tensor"),
        P("pipe", "tensor", None),
        P("pipe", None, "tensor"),
        P("pipe", None, "tensor"),
        P("pipe", "tensor", None),
        P("pipe", None, None),
    )
    out_specs = P("pipe", None, None, None)
    return jax.shard_map(body, mesh=mesh, in_specs=in_specs, out_specs=out_specs, check_vma=False)
```

profile of v0, /device:TPU:0, one launch (start us, length us, event | category | flops | bytes accessed | tf_op | source)
XLA Modules:
  0.0 962.4 jit_solution(4776176420488982353)
XLA Ops:
  6.5 7.1 broadcast_select_fusion.1
  13.7 2.0 copy-done.4
  15.7 3.8 copy.57
  19.7 289.4 %all-gather.3.cloned.1.call-done = bf16[1024,8192]{1,0:T(8,128)(2,1)} async-done(((bf16[1024,2048]{1,0:T(8,128)(2,1)}), bf16[1024,8192]{1,0:T(8,128)(2,1)}) %all-gather.3.cloned.1.call-update) | async-done | bytes 16777232 | tf_op jit(solution)/shard_map/all_gather | solution.py:45
  309.1 44.5 %fusion.13 = bf16[1024,2048]{1,0:T(8,128)(2,1)} fusion(bf16[1024,8192]{1,0:T(8,128)(2,1)} %all-gather.3.cloned.1.call-done, bf16[1,2048,8192]{2,1,0:T(8,128)(2,1)} %param.11), kind=kOutput, calls=%fused_computation.23 | convolution fusion | flops 34361835520 | bytes 54525952 | tf_op jit(solution)/shard_map/dot_general | solution.py:49
  353.7 13.6 %convert_multiply_fusion = (f32[2,512,2048]{2,1,0:T(8,128)}, f32[2,512,2048]{2,1,0:T(8,128)}) fusion(bf16[2,512,2048]{2,1,0:T(8,128)(2,1)} %bitcast.61, bf16[1,2,512,2048]{3,2,1,0:T(8,128)(2,1)} %param.9, bf16[1,2,512,2048]{3,2,1,0:T(8,128)(2,1)} %param.10), kind=kLoop, calls=%fused_computation.3 | loop fusion | flops 10485760 | bytes 29360128 | tf_op jit(solution)/shard_map/mul | solution.py:60
  369.5 1.7 slice.18
  372.3 1.5 collective-permute-start.1
  374.4 4.0 pad_maximum_fusion.1
  378.4 7.6 copy.69
  386.0 4.5 pad.clone
  390.6 8.8 fusion.4
  399.4 10.1 %broadcast_select_fusion.2 = f32[16,65,2048]{2,0,1:T(8,128)S(1)} fusion(pred[16,65]{0,1:T(8,128)(4,1)S(1)} %copy-done.9, f32[2,8,71,2048]{3,0,2,1:T(2,128)S(1)} %fusion.4, f32[1,7,2048]{2,0,1:T(1,128)S(1)} %copy-done.8), kind=kOutput, calls=%fused_computation.22 | convolution fusion | flops 181043200 | bytes 17884176 | tf_op jit(solution)/shard_map/conv_general_dilated | solution.py:16
  409.5 8.7 copy.60
  418.2 9.8 %reshape.40 = f32[2,520,2048]{2,1,0:T(8,128)} reshape(f32[16,65,2048]{2,1,0:T(8,128)} %copy.60) | data formatting | bytes 17039360 | tf_op jit(solution)/shard_map/conv_general_dilated | solution.py:16
  428.0 7.8 slice.14
  435.8 1.6 copy_convert_fusion
  437.4 9.0 pad_maximum_fusion
  446.4 121.0 %fusion.10 = bf16[2,512,2048]{2,0,1:T(2,128)(2,1)} fusion(f32[2,512,2048]{2,1,0:T(8,128)} %slice.14, bf16[2,512,2048]{2,0,1:T(2,128)(2,1)} %copy-done.4, f32[2,639,2048]{2,1,0:T(8,128)} %pad_maximum_fusion, f32[128,1,2048]{2,0,1:T(8,128)S(1)} %bitcast.53), kind=kOutput, calls=%fused_computation.19 | convolution fusion | flops 3229614080 | bytes 28295168 | tf_op jit(solution)/shard_map/conv_general_dilated | solution.py:16
  567.5 1.4 collective-permute-start.2
  568.9 2.3 fusion.8
  571.2 1.4 fusion.23
  573.6 3.3 collective-permute-done.2
  577.0 11.0 %broadcast_select_fusion = bf16[2,512,2048]{2,0,1:T(2,128)(2,1)} fusion(bf16[2,512,2048]{2,0,1:T(2,128)(2,1)} %collective-permute-done.2, pred[]{:T(512)S(6)} %eq.10, bf16[2,512,2048]{2,1,0:T(8,128)(2,1)} %param.8), kind=kLoop, calls=%fused_computation.20 | loop fusion | flops 2097152 | bytes 12582913 | tf_op jit(solution)/shard_map/jit(_where)/select_n | solution.py:102
  587.9 6.2 copy.67
  594.5 11.0 %fusion.18 = f32[2,512,64]{1,2,0:T(8,128)S(1)} fusion(bf16[2,512,8192]{2,1,0:T(8,128)(2,1)} %bitcast.57, bf16[1,8192,64]{1,2,0:T(8,128)(2,1)S(1)} %copy-done.5), kind=kOutput, calls=%fused_computation.27 | convolution fusion | flops 1073741824 | bytes 18087936 | tf_op jit(solution)/shard_map/dot_general | solution.py:52
  605.5 7.9 all-reduce.4.cloned.1.call-done
  613.4 1.9 convolution_multiply_fusion
  615.3 286.3 %all-gather.5.cloned.1.call-done = bf16[1024,8192]{1,0:T(8,128)(2,1)} async-done(((bf16[1024,2048]{1,0:T(8,128)(2,1)}), bf16[1024,8192]{1,0:T(8,128)(2,1)}) %all-gather.5.cloned.1.call-update) | async-done | bytes 16777232 | tf_op jit(solution)/shard_map/all_gather | solution.py:45
  901.6 11.1 %fusion.20 = f32[2,512,64]{1,2,0:T(8,128)S(1)} fusion(bf16[2,512,8192]{2,1,0:T(8,128)(2,1)} %bitcast.58, bf16[1,8192,64]{1,2,0:T(8,128)(2,1)S(1)} %copy-done.5), kind=kOutput, calls=%fused_computation.29 | convolution fusion | flops 1073741824 | bytes 18087936 | tf_op jit(solution)/shard_map/dot_general | solution.py:52
  913.7 40.4 %all-reduce.6.cloned.1.call-done = (f32[2,64,64]{2,1,0:T(8,128)}, f32[2,64,64]{2,1,0:T(8,128)}) async-done(((f32[2,64,64]{2,1,0:T(8,128)}, f32[2,64,64]{2,1,0:T(8,128)}), (f32[2,64,64]{2,1,0:T(8,128)}, f32[2,64,64]{2,1,0:T(8,128)})) %all-reduce.6.cloned.1.call-update) | async-done | bytes 65552 | tf_op jit(solution)/shard_map/psum | solution.py:81
  954.1 1.5 select_bitcast_fusion
  (36 shorter events, 6.5 us)
Async XLA Ops:
  6.5 439.9 %copy-start = (f32[1,128,2048]{2,1,0:T(8,128)S(1)}, f32[1,128,2048]{2,1,0:T(8,128)}, u32[]{:S(2)}) copy-start(f32[1,128,2048]{2,1,0:T(8,128)} %param.13) | copy-start | bytes 3145732
  6.5 302.6 %all-gather.3.cloned.1.call-start = ((), (), s32[]{:S(2)}) async-start(), calls=%async_computation.1 | async-start | bytes 20971520 | tf_op jit(solution)/shard_map/all_gather | solution.py:45
  13.7 2.0 copy-start.4
  19.5 593.9 %all-reduce.4.cloned.1.call-start = ((), (), s32[]{:S(2)}) async-start(), calls=%async_computation | async-start | bytes 524288 | tf_op jit(solution)/shard_map/psum | solution.py:77
  368.2 6.1 collective-permute-start
  372.3 63.5 %collective-permute-start.1 = (bf16[2,127,2048]{2,0,1:T(2,128)(2,1)S(1)}, bf16[2,127,2048]{2,0,1:T(2,128)(2,1)}, u32[]{:S(2)}, u32[]{:S(2)}) collective-permute-start(bf16[2,127,2048]{2,0,1:T(2,128)(2,1)S(1)} %copy.62), channel_id=1, source_target_pairs={{1,0},{2,1},{3,2},{5,4},{6,5},{7,6},{9,8},{10,9},{11,10},{13,12},{... | collective-permute-start | bytes 3121160 | tf_op jit(solution)/shard_map/ppermute | solution.py:12
  390.6 8.8 copy-start.8
  390.6 8.8 copy-start.9
  446.4 122.5 %copy-start.2 = (bf16[1,2,512,2048]{3,2,1,0:T(8,128)(2,1)S(1)}, bf16[1,2,512,2048]{3,2,1,0:T(8,128)(2,1)}, u32[]{:S(2)}) copy-start(bf16[1,2,512,2048]{3,2,1,0:T(8,128)(2,1)} %param.10) | copy-start | bytes 12582916
  446.4 122.5 %copy-start.3 = (bf16[1,2,512,2048]{3,2,1,0:T(8,128)(2,1)S(1)}, bf16[1,2,512,2048]{3,2,1,0:T(8,128)(2,1)}, u32[]{:S(2)}) copy-start(bf16[1,2,512,2048]{3,2,1,0:T(8,128)(2,1)} %param.9) | copy-start | bytes 12582916
  567.4 3.7 copy-start.7
  567.5 9.5 collective-permute-start.2
  573.4 328.2 %all-gather.5.cloned.1.call-start = ((), (), s32[]{:S(2)}) async-start(), calls=%async_computation.2 | async-start | bytes 20971520 | tf_op jit(solution)/shard_map/all_gather | solution.py:45
  587.9 6.6 copy-start.5
  594.2 359.9 %all-reduce.6.cloned.1.call-start = ((), (), s32[]{:S(2)}) async-start(), calls=%async_computation.3 | async-start | bytes 262144 | tf_op jit(solution)/shard_map/psum | solution.py:81
  901.6 54.0 %copy-start.1 = (f32[1,128,2048]{2,1,0:T(8,128)S(1)}, f32[1,128,2048]{2,1,0:T(8,128)}, u32[]{:S(2)}) copy-start(f32[1,128,2048]{2,1,0:T(8,128)} %param.13) | copy-start | bytes 3145732
  901.6 11.1 %copy-start.6 = (f32[2,512,64]{1,2,0:T(8,128)S(1)}, f32[2,512,64]{1,2,0:T(8,128)}, u32[]{:S(2)}) copy-start(f32[2,512,64]{1,2,0:T(8,128)} %all-reduce.4.cloned.1.call-done) | copy-start | bytes 786436
Sparse Core Ops, SparseCore 0:
  19.6 289.4 all-gather.2
  573.5 39.8 all-reduce.3
  615.0 286.5 all-gather.4
  913.8 40.2 all-reduce.5
where the time goes:
time: 968 us; the launch traced here: 962 us
  waiting for transfers between devices  628 us (65%)
  matrix products  202 us (21%)
  other arithmetic  58.9 us (6%)
  local copies, waits for them, and re-layouts  54.9 us (6%)
  between operations  13.6 us (1%)
    all_gather x2, waiting for transfers between devices, layer_pass(): shard_piece = lax.all_gather(flat_grad, 'tensor', axis=1, tiled=True)  576 us
    conv_general_dilated x2, matrix products, adjoint_filter(): lax.conv_general_dilated(extended, filter_taps[:, None, :], (1,), 'VALID'...  131 us
    dot_general x1, matrix products, layer_pass(): lax.dot_general(shard_piece, weight_cols, (((1,), (1,)), ((), ())), prefe...  44.5 us
    psum x1, waiting for transfers between devices, layer_pass(): layer_grads = lax.psum(local_grads, 'dp')  40.4 us
    conv_general_dilated x4, local copies, waits for them, and re-layouts, adjoint_filter(): lax.conv_general_dilated(extended, filter_taps[:, None, :], (1,), 'VALID'...  26.3 us
    dot_general x2, matrix products, layer_pass(): jnp.dot(shard_piece, basis_rows, preferred_element_type=jnp.float32)  22 us
  transfers between devices with their start and end apart: 7, of which 6 were waited for; matrix products, arithmetic and copies ran while one was open for 10% of the time, Pallas kernels for 0%

commit v1 on v0

v1 whole, which is shorter than its diff:
```python
import functools
import math

import jax
import jax.numpy as jnp
import numpy as np
from jax import lax
from jax.experimental import pallas as pl
from jax.experimental.pallas import tpu as pltpu
from jax.sharding import PartitionSpec as P

MESH = pl.DeviceIdType.MESH
BLOCK = 256
NT = (((1,), (1,)), ((), ()))


def passed_along(array, axis, by):
    devices = lax.axis_size(axis)
    pairs = [(i, i + by) for i in range(devices) if 0 <= i + by < devices]
    return lax.ppermute(array, axis, pairs)


def transforms(taps):
    size = BLOCK + taps
    freq = 2.0 * np.pi * (np.arange(size // 2) + 0.5) / size

    def table(times, sign):
        angle = freq[:, None] * times[None, :]
        return np.concatenate([np.cos(angle), sign * np.sin(angle)], axis=0)

    ahead = table(np.arange(BLOCK), -1.0).astype(jnp.bfloat16)
    filters = table(np.arange(taps), 1.0).astype(np.float32)
    back = (table(np.arange(-taps, BLOCK), -1.0) * (2.0 / size)).astype(np.float32)
    return ahead, filters, back


def kernel(
    n, parts, tile,
    x_hbm, w_hbm, ss_hbm, sm_hbm, po_hbm, fm_ref, fs_ref, ahead_ref, ftab_ref,
    z_ref, oc_ref,
    held, acc, wbuf, ss, sm, p0, p1, spec, xs, ws, ls, send_l, send_r, recv, psend, precv,
):
    z = lax.axis_index("tensor")
    top = lax.axis_index("pipe") == lax.axis_size("pipe") - 1
    has_left, has_right = z > 0, z < n - 1
    rows, depth = held.shape[1], held.shape[2]
    width = x_hbm.shape[1]
    half = spec.shape[1]
    tiles = spec.shape[2] // tile
    barrier = pltpu.get_barrier_semaphore()
    po_rows = pl.ds(pl.multiple_of(z * width, width), width)

    p0_copy = pltpu.make_async_remote_copy(
        src_ref=po_hbm.at[po_rows], dst_ref=p0, send_sem=psend, recv_sem=precv,
        device_id={"pipe": 1}, device_id_type=MESH,
    )

    def to_left(i):
        return pltpu.make_async_remote_copy(
            src_ref=held.at[i], dst_ref=held.at[i], send_sem=send_l.at[i], recv_sem=recv.at[i],
            device_id={"tensor": z - 1}, device_id_type=MESH,
        )

    def to_right(i):
        return pltpu.make_async_remote_copy(
            src_ref=held.at[i], dst_ref=held.at[i], send_sem=send_r.at[i], recv_sem=recv.at[i],
            device_id={"tensor": z + 1}, device_id_type=MESH,
        )

    def own_copy(q):
        return pltpu.make_async_copy(
            x_hbm.at[:, pl.ds(pl.multiple_of(q * depth, depth), depth)], held.at[z * parts + q], xs.at[q]
        )

    def weight_copy(i, side):
        return pltpu.make_async_copy(
            w_hbm.at[:, pl.ds(pl.multiple_of(i * depth, depth), depth)], wbuf.at[side], ws.at[side]
        )

    def multiply(i, side):
        @pl.loop(0, tiles)
        def _(c):
            weights = wbuf[side, pl.ds(pl.multiple_of(c * tile, tile), tile), :]
            acc[c] += lax.dot_general(held[i], weights, NT, preferred_element_type=jnp.float32)

    @pl.when(jnp.logical_not(top))
    def _():
        z_ref[...] = jnp.zeros_like(z_ref)
        oc_ref[...] = jnp.zeros_like(oc_ref)
        pl.semaphore_wait(barrier, 1)
        p0_copy.start()
        p0_copy.wait_send()

    @pl.when(top)
    def _():
        for q in range(parts):
            own_copy(q).start()
        saved_copies = (
            pltpu.make_async_copy(ss_hbm, ss, ls.at[0]),
            pltpu.make_async_copy(sm_hbm, sm, ls.at[1]),
        )
        p1_copy = pltpu.make_async_copy(po_hbm.at[po_rows], p1, ls.at[2])
        pl.semaphore_signal(barrier, inc=1, device_id={"pipe": 0}, device_id_type=MESH)

        @pl.when(has_left)
        def _():
            pl.semaphore_signal(barrier, inc=1, device_id={"tensor": z - 1}, device_id_type=MESH)

        @pl.when(has_right)
        def _():
            pl.semaphore_signal(barrier, inc=1, device_id={"tensor": z + 1}, device_id_type=MESH)

        pl.semaphore_wait(barrier, jnp.minimum(z, 1) + jnp.minimum(n - 1 - z, 1))

        for q in range(parts):
            own_copy(q).wait()

            @pl.when(has_left)
            def _():
                to_left(z * parts + q).start()

            @pl.when(has_right)
            def _():
                to_right(z * parts + q).start()

        p1_copy.start()
        for copy in saved_copies:
            copy.start()
        z_ref[...] = jnp.zeros_like(z_ref)
        oc_ref[...] = jnp.zeros_like(oc_ref)
        acc[...] = jnp.zeros_like(acc)

        @pl.loop(0, tiles)
        def _(c):
            cols = pl.ds(pl.multiple_of(c * tile, tile), tile)
            spec[0:2, :, cols] = jnp.dot(
                ftab_ref[...], fm_ref[:, cols], precision=lax.Precision.HIGHEST,
                preferred_element_type=jnp.float32,
            ).reshape(2, half, tile)
            for part in range(2):
                total = jnp.zeros((half, tile), jnp.float32)
                for j in range(fs_ref.shape[0]):
                    total += ftab_ref[part * half : (part + 1) * half, j : j + 1] * fs_ref[j : j + 1, cols]
                spec[2 + part, :, cols] = total

        p1_copy.wait()
        p0_copy.wait_recv()

        @pl.loop(0, parts)
        def _(q):
            i = z * parts + q
            weight_copy(i, 0).start()
            mine = pl.ds(pl.multiple_of(q * depth, depth), depth)
            oc_ref[0] += jnp.dot(held[i], p0[mine, :], preferred_element_type=jnp.float32)
            oc_ref[1] += jnp.dot(held[i], p1[mine, :], preferred_element_type=jnp.float32)
            weight_copy(i, 0).wait()
            multiply(i, 0)

        @pl.loop(1, n)
        def _(k):
            from_left, from_right = z >= k, z + k < n

            @pl.loop(0, parts)
            def _(q):
                i_left, i_right = (z - k) * parts + q, (z + k) * parts + q

                @pl.when(from_left)
                def _():
                    weight_copy(i_left, 0).start()

                @pl.when(from_right)
                def _():
                    weight_copy(i_right, 1).start()

                @pl.when(from_left)
                def _():
                    to_right(i_left).wait_recv()

                    @pl.when(has_right)
                    def _():
                        to_right(i_left).start()

                @pl.when(from_right)
                def _():
                    to_left(i_right).wait_recv()

                    @pl.when(has_left)
                    def _():
                        to_left(i_right).start()

                @pl.when(from_left)
                def _():
                    weight_copy(i_left, 0).wait()
                    multiply(i_left, 0)

                @pl.when(from_right)
                def _():
                    weight_copy(i_right, 1).wait()
                    multiply(i_right, 1)

        for copy in saved_copies:
            copy.wait()

        @pl.loop(0, tiles)
        def _(c):
            cols = pl.ds(pl.multiple_of(c * tile, tile), tile)
            for b in range(rows // BLOCK):
                span = slice(b * BLOCK, (b + 1) * BLOCK)
                back = acc[c, span, :].astype(jnp.bfloat16).astype(jnp.float32)
                gate_medium = (back * ss[span, cols].astype(jnp.float32)).astype(jnp.bfloat16)
                gate_short = (back * sm[span, cols].astype(jnp.float32)).astype(jnp.bfloat16)
                gm = jnp.dot(ahead_ref[...], gate_medium, preferred_element_type=jnp.float32)
                gs = jnp.dot(ahead_ref[...], gate_short, preferred_element_type=jnp.float32)
                m_re, m_im = spec[0, :, cols], spec[1, :, cols]
                s_re, s_im = spec[2, :, cols], spec[3, :, cols]
                real = m_re * gm[:half] - m_im * gm[half:] + s_re * gs[:half] - s_im * gs[half:]
                imag = m_re * gm[half:] + m_im * gm[:half] + s_re * gs[half:] + s_im * gs[:half]
                basis = p0[cols, :]
                base = 2 * half * b
                z_ref[base : base + half, :] += jnp.dot(
                    real.astype(jnp.bfloat16), basis, preferred_element_type=jnp.float32
                )
                z_ref[base + half : base + 2 * half, :] += jnp.dot(
                    imag.astype(jnp.bfloat16), basis, preferred_element_type=jnp.float32
                )

        @pl.loop(0, n)
        def _(s):
            @pl.loop(0, parts)
            def _(q):
                i = s * parts + q

                @pl.when(jnp.logical_and(has_left, s >= z))
                def _():
                    to_left(i).wait_send()

                @pl.when(jnp.logical_and(has_right, s <= z))
                def _():
                    to_right(i).wait_send()


def back_pass(x, weight, ss, sm, basis, fm, fs, ahead, ftab):
    n = lax.axis_size("tensor")
    rows, width = x.shape
    channels = weight.shape[0]
    rank = basis.shape[1]
    depth = min(512, width)
    parts = width // depth
    tile = min(256, channels)
    size = ahead.shape[0]
    any_spec = pl.BlockSpec(memory_space=pl.ANY)
    vmem = pl.BlockSpec(memory_space=pltpu.VMEM)
    dma = pltpu.SemaphoreType.DMA
    return pl.pallas_call(
        functools.partial(kernel, n, parts, tile),
        out_shape=(
            jax.ShapeDtypeStruct((rows // BLOCK * size, rank), jnp.float32),
            jax.ShapeDtypeStruct((2, rows, rank), jnp.float32),
        ),
        in_specs=[any_spec] * 5 + [vmem] * 4,
        out_specs=(vmem, vmem),
        scratch_shapes=[
            pltpu.VMEM((n * parts, rows, depth), jnp.bfloat16),
            pltpu.VMEM((channels // tile, rows, tile), jnp.float32),
            pltpu.VMEM((2, channels, depth), jnp.bfloat16),
            pltpu.VMEM((rows, channels), jnp.bfloat16),
            pltpu.VMEM((rows, channels), jnp.bfloat16),
            pltpu.VMEM((width, rank), jnp.bfloat16),
            pltpu.VMEM((width, rank), jnp.bfloat16),
            pltpu.VMEM((4, size // 2, channels), jnp.float32),
            dma((parts,)), dma((2,)), dma((3,)),
            dma((n * parts,)), dma((n * parts,)), dma((n * parts,)),
            dma, dma,
        ],
        cost_estimate=pl.CostEstimate(
            flops=2 * rows * channels * width * n, bytes_accessed=2 * channels * width * n, transcendentals=0
        ),
        compiler_params=pltpu.CompilerParams(
            collective_id=0, has_side_effects=True, vmem_limit_bytes=60 * 2**20
        ),
        name="back_pass",
    )(x, weight, ss, sm, basis, fm, fs, ahead, ftab)


def body(
    cotangent, saved_short, saved_medium, out_weight, short_filter, medium_filter, proj_in, proj_out
):
    section = lax.axis_index("pipe")
    micro, seq_dev, width = cotangent.shape
    rows = micro * seq_dev
    rank = proj_in.shape[2]
    norm_factor = 1.0 / math.sqrt(seq_dev * lax.axis_size("dp"))
    taps = medium_filter.shape[1]
    ahead, ftab, back = transforms(taps)
    ss = saved_short.reshape(rows, -1)
    sm = saved_medium.reshape(rows, -1)

    spectra, out_parts = back_pass(
        cotangent.reshape(rows, width), out_weight[0], ss, sm, proj_out[0],
        medium_filter[0], short_filter[0], jnp.asarray(ahead), jnp.asarray(ftab),
    )

    gated = (ss.astype(jnp.float32) * sm.astype(jnp.float32)).astype(jnp.bfloat16)
    in_part = jnp.dot(gated, proj_in[0], preferred_element_type=jnp.float32)
    in_side = lax.psum(in_part, "tensor").reshape(micro, seq_dev, rank)
    before = passed_along(in_side[:, seq_dev - taps :], "dp", 1)
    below = passed_along(jnp.concatenate([before, in_side], axis=1), "pipe", 1)
    windows = jnp.stack(
        [below[:, b * BLOCK : (b + 1) * BLOCK + taps] for b in range(seq_dev // BLOCK)], axis=1
    )
    high = lax.Precision.HIGHEST
    turned = jnp.einsum("kt,mbtr->mbkr", jnp.asarray(back), windows, precision=high)

    spectra = spectra.reshape(micro, seq_dev // BLOCK, -1, rank)
    out_parts = out_parts.reshape(2, micro, seq_dev, rank)
    lower = jnp.einsum("mbkr,mbkq->mrq", turned, spectra, precision=high)
    lower += jnp.einsum("mtr,mtq->mrq", below[:, taps:], out_parts[0], precision=high)
    upper = jnp.einsum("mtr,mtq->mrq", in_side, out_parts[1], precision=high)
    both = lax.psum(jnp.stack([lower, upper]) * norm_factor, ("pipe", "tensor", "dp"))
    return lax.dynamic_index_in_dim(both, section, 0, keepdims=True)


def solution(mesh):
    in_specs = (
        P(None, "dp", "tensor"),
        P("pipe", None, "dp", "tensor"),
        P("pipe", None, "dp", "tensor"),
        P("pipe", "tensor", None),
        P("pipe", None, "tensor"),
        P("pipe", None, "tensor"),
        P("pipe", "tensor", None),
        P("pipe", None, None),
    )
    out_specs = P("pipe", None, None, None)
    return jax.shard_map(body, mesh=mesh, in_specs=in_specs, out_specs=out_specs, check_vma=False)
```

time: 968 us -> 348 us (0.36)
  waiting for transfers between devices: 628 us -> 157 us
  matrix products: 202 us -> 3.79 us
  starting transfers between devices: 4.97 us -> 156 us
  other arithmetic: 58.9 us -> 6.12 us
  local copies, waits for them, and re-layouts: 54.9 us -> 6.81 us
    all_gather x2 -> x0, waiting for transfers between devices: 576 us -> none  [layer_pass(): shard_piece = lax.all_gather(flat_grad, 'tensor', axis=1, tiled=True)]
    ppermute x3 -> x2, starting transfers between devices: 4.2 us -> 156 us  [passed_along(): return lax.ppermute(array, axis, pairs)]
    conv_general_dilated x2 -> x0, matrix products: 131 us -> none  [adjoint_filter(): lax.conv_general_dilated(extended, filter_taps[:, None, :], (1,), 'VALID'...]
    psum x2, waiting for transfers between devices: 48.3 us -> 156 us  [the longest x1 121 us: body(): lax.psum(jnp.stack([lower, upper]) * norm_factor, ('pipe', 'tensor', 'dp'))]
    dot_general x6 -> x5, matrix products: 70.9 us -> 3.79 us  [the longest x1 1.4 us: body(): in_part = jnp.dot(gated, proj_in[0], preferred_element_type=jnp.float32)]
    conv_general_dilated x4 -> x0, local copies, waits for them, and re-layouts: 26.3 us -> none  [adjoint_filter(): lax.conv_general_dilated(extended, filter_taps[:, None, :], (1,), 'VALID'...]
    select_n x2 -> x0, other arithmetic: 18.1 us -> none  [body(): incoming = jnp.where(is_top, cotangent, received)]
    concatenate x2 -> x1, other arithmetic: 13 us -> 0.02 us  [body(): below = passed_along(jnp.concatenate([before, in_side], axis=1), 'pipe', 1)]
  transfers between devices with their start and end apart: 7 -> 4, of which waited for: 6 -> 2; matrix products, arithmetic and copies ran while one was open for 10% -> 1% of each run, Pallas kernels for 0% -> 1%
where the time goes in v1:
time: 348 us; the launch traced here: 347 us
  waiting for transfers between devices  157 us (45%)
  starting transfers between devices  156 us (45%)
  between operations  13.6 us (4%)
  local copies, waits for them, and re-layouts  6.81 us (2%)
  other arithmetic  6.12 us (2%)
  Pallas kernels  5.06 us (1%)
  matrix products  3.79 us (1%)
    ppermute x2, starting transfers between devices, passed_along(): return lax.ppermute(array, axis, pairs)  156 us
    psum x1, waiting for transfers between devices, body(): lax.psum(jnp.stack([lower, upper]) * norm_factor, ('pipe', 'tensor', 'dp'))  121 us
    psum x1, waiting for transfers between devices, body(): in_side = lax.psum(in_part, 'tensor').reshape(micro, seq_dev, rank)  35.7 us
  transfers between devices with their start and end apart: 4, of which 2 were waited for; matrix products, arithmetic and copies ran while one was open for 1% of the time, Pallas kernels for 1%

profile of v1, /device:TPU:0, one launch (start us, length us, event | category | flops | bytes accessed | tf_op | source)
XLA Modules:
  0.0 347.4 jit_solution(9351214319446874647)
XLA Ops:
  6.5 0.0 copy-start
  6.5 0.0 all-reduce.3.cloned.1.call-start
  6.5 5.4 %multiply_convert_fusion = bf16[1,2,512,2048]{3,2,1,0:T(8,128)(2,1)S(1)} fusion(bf16[1,2,512,2048]{3,2,1,0:T(8,128)(2,1)} %param.13, bf16[1,2,512,2048]{3,2,1,0:T(8,128)(2,1)} %param.12), kind=kLoop, calls=%fused_computation | loop fusion | flops 8388608 | bytes 12582912 | tf_op jit(solution)/shard_map/convert_element_type | solution.py:303
  12.0 0.0 copy-start.2
  12.0 0.0 copy-done
  12.0 0.0 copy-start.5
  12.0 1.4 fusion.3
  13.4 0.7 copy.29
  14.1 0.0 all-reduce.3.cloned.1.call-update
  14.2 0.0 all-reduce.5.cloned.1.call-start
  14.2 1.8 copy.13
  16.0 0.0 copy-done.5
  16.0 0.7 copy.30
  16.7 35.7 %all-reduce.3.cloned.1.call-done = f32[2,512,64]{1,2,0:T(8,128)} async-done(((f32[2,512,64]{1,2,0:T(8,128)}), f32[2,512,64]{1,2,0:T(8,128)}) %all-reduce.3.cloned.1.call-update) | async-done | bytes 262160 | tf_op jit(solution)/shard_map/psum | solution.py:305
  52.3 0.8 slice.26
  53.2 3.4 collective-permute-start
  56.5 0.0 copy-start.1
  56.5 5.1 %back_pass.1 = (f32[1536,64]{1,0:T(8,128)}, f32[2,1024,64]{2,1,0:T(8,128)}) custom-call(bf16[1024,2048]{1,0:T(8,128)(2,1)} %bitcast.54, bf16[2048,8192]{1,0:T(8,128)(2,1)} %bitcast.53, bf16[1024,2048]{1,0:T(8,128)(2,1)} %bitcast.45, bf16[1024,2048]{1,0:T(8,128)(2,1)} %bitcast.44, bf16[8192,64]{1,0:T(8,128)(2,1)} %bitcast.46, f32[128,2048]{1,0:T(8,128)} %bitcast.55, ...), custom_call_target="tpu_custom_call" | custom-call | flops 34359738368 | bytes 33554432 | tf_op jit(solution)/shard_map/back_pass/pallas_call | solution.py:254
  61.6 0.0 copy-start.4
  61.6 0.0 copy-start.3
  61.6 0.0 collective-permute-done
  61.7 152.2 %collective-permute-start.1 = (f32[2,640,64]{1,2,0:T(8,128)S(1)}, f32[2,640,64]{1,2,0:T(8,128)S(1)}, u32[]{:S(2)}, u32[]{:S(2)}) collective-permute-start(f32[2,640,64]{1,2,0:T(8,128)S(1)} %pad_maximum_fusion.1), channel_id=1, source_target_pairs={{0,16},{1,17},{2,18},{3,19},{4,20},{5,21},{6,22},{7,23},{8,24},{9,... | collective-permute-start | bytes 983048 | tf_op jit(solution)/shard_map/ppermute | solution.py:20
  213.9 1.3 fusion.5
  215.1 0.4 convolution_bitcast_fusion.1
  215.6 0.0 collective-permute-done.1
  215.6 0.9 convolution_bitcast_fusion
  216.6 0.6 convolution_bitcast_fusion.2
  217.2 0.4 fusion
  217.6 0.7 maximum_multiply_fusion
  218.3 0.0 all-reduce.5.cloned.1.call-update
  218.3 120.8 %all-reduce.5.cloned.1.call-done = f32[2,2,64,64]{3,2,1,0:T(8,128)} async-done(((f32[2,2,64,64]{3,2,1,0:T(8,128)}), f32[2,2,64,64]{3,2,1,0:T(8,128)}) %all-reduce.5.cloned.1.call-update) | async-done | bytes 65552 | tf_op jit(solution)/shard_map/psum | solution.py:319
  339.1 1.5 constant_dynamic-slice_fusion
  (6 shorter events, 0.1 us)
Async XLA Ops:
  6.5 5.4 %copy-start = (bf16[1,2048,64]{1,2,0:T(8,128)(2,1)S(1)}, bf16[1,2048,64]{1,2,0:T(8,128)(2,1)}, u32[]{:S(2)}) copy-start(bf16[1,2048,64]{1,2,0:T(8,128)(2,1)} %param.17) | copy-start | bytes 786436
  6.5 45.8 %all-reduce.3.cloned.1.call-start = ((), (), s32[]{:S(2)}) async-start(), calls=%async_computation | async-start | bytes 524288 | tf_op jit(solution)/shard_map/psum | solution.py:305
  12.0 2.2 copy-start.2
  12.0 4.0 %copy-start.5 = (f32[1,7,2048]{2,0,1:T(1,128)S(1)}, f32[1,7,2048]{2,0,1:T(1,128)}, u32[]{:S(2)}) copy-start(f32[1,7,2048]{2,0,1:T(1,128)} %param.15) | copy-start | bytes 172036
  14.2 325.0 %all-reduce.5.cloned.1.call-start = ((), (), s32[]{:S(2)}) async-start(), calls=%async_computation.1 | async-start | bytes 262144 | tf_op jit(solution)/shard_map/psum | solution.py:319
  53.2 8.5 %collective-permute-start = (f32[2,128,64]{1,2,0:T(8,128)S(1)}, f32[2,128,64]{1,2,0:T(8,128)S(1)}, u32[]{:S(2)}, u32[]{:S(2)}) collective-permute-start(f32[2,128,64]{1,2,0:T(8,128)S(1)} %slice.26), channel_id=1, source_target_pairs={{0,1},{1,2},{2,3},{4,5},{5,6},{6,7},{8,9},{9,10},{10,11},{12,13},{... | collective-permute-start | bytes 196616 | tf_op jit(solution)/shard_map/ppermute | solution.py:20
  56.5 5.1 %copy-start.1 = (f32[2,512,64]{1,2,0:T(8,128)S(1)}, f32[2,512,64]{1,2,0:T(8,128)}, u32[]{:S(2)}) copy-start(f32[2,512,64]{1,2,0:T(8,128)} %all-reduce.3.cloned.1.call-done) | copy-start | bytes 786436
  61.6 154.0 %copy-start.4 = (f32[384,384,1,1]{1,0,3,2:T(8,128)S(1)}, f32[384,384,1,1]{1,0,3,2:T(8,128)}, u32[]{:S(2)}) copy-start(f32[384,384,1,1]{1,0,3,2:T(8,128)} %constant.30) | copy-start | bytes 1769476
  61.6 154.9 %copy-start.3 = (f32[1536,64]{1,0:T(8,128)S(1)}, f32[1536,64]{1,0:T(8,128)}, u32[]{:S(2)}) copy-start(f32[1536,64]{1,0:T(8,128)} %get-tuple-element.7) | copy-start | bytes 1179652
  61.7 153.9 %collective-permute-start.1 = (f32[2,640,64]{1,2,0:T(8,128)S(1)}, f32[2,640,64]{1,2,0:T(8,128)S(1)}, u32[]{:S(2)}, u32[]{:S(2)}) collective-permute-start(f32[2,640,64]{1,2,0:T(8,128)S(1)} %pad_maximum_fusion.1), channel_id=1, source_target_pairs={{0,16},{1,17},{2,18},{3,19},{4,20},{5,21},{6,22},{7,23},{8,24},{9,... | collective-permute-start | bytes 983048 | tf_op jit(solution)/shard_map/ppermute | solution.py:20
Sparse Core Ops, SparseCore 0:
  14.3 38.0 all-reduce.2
  218.4 120.6 all-reduce.4

commit v2 on v1

v2 whole, which is shorter than its diff:
```python
import functools
import math

import jax
import jax.numpy as jnp
import numpy as np
from jax import lax
from jax.experimental import pallas as pl
from jax.experimental.pallas import tpu as pltpu
from jax.sharding import PartitionSpec as P

MESH = pl.DeviceIdType.MESH
BLOCK = 256
NT = (((1,), (1,)), ((), ()))


def transforms(taps):
    size = BLOCK + taps
    freq = 2.0 * np.pi * (np.arange(size // 2) + 0.5) / size

    def table(times, sign):
        angle = freq[:, None] * times[None, :]
        return np.concatenate([np.cos(angle), sign * np.sin(angle)], axis=0)

    ahead = table(np.arange(BLOCK), -1.0).astype(jnp.bfloat16)
    filters = table(np.arange(taps), 1.0).astype(np.float32)
    back = (table(np.arange(-taps, BLOCK), -1.0) * (2.0 / size)).astype(np.float32)
    return ahead, filters, back


def kernel(
    n, parts, tile,
    x_hbm, w_hbm, ss_hbm, sm_hbm, po_hbm, pi_ref, fm_ref, fs_ref, ahead_ref, ftab_ref, back_ref,
    out_ref,
    held, acc, wbuf, ss, sm, p0, p1, spec, z_ref, oc_ref,
    in_own, in_sum, in_low, in_up, in_pad, turned, lower, upper, red_dp, red_z, final,
    xs, ws, ls, send_l, send_r, recv, psend, precv,
    in_send, low_recv, up_recv, halo_send, halo_recv,
    dp_send, dp_recv, z_send, z_recv, fin_send, fin_recv,
):
    z = lax.axis_index("tensor")
    y = lax.axis_index("dp")
    dps = red_dp.shape[0]
    micro, rank, padded = in_pad.shape
    taps = padded - held.shape[1] // micro
    seq = padded - taps
    scale = 1.0 / math.sqrt(seq * dps)
    high = lax.Precision.HIGHEST
    top = lax.axis_index("pipe") == lax.axis_size("pipe") - 1
    has_left, has_right = z > 0, z < n - 1
    rows, depth = held.shape[1], held.shape[2]
    width = x_hbm.shape[1]
    half = spec.shape[1]
    tiles = spec.shape[2] // tile
    barrier = pltpu.get_barrier_semaphore()
    po_rows = pl.ds(pl.multiple_of(z * width, width), width)

    p0_copy = pltpu.make_async_remote_copy(
        src_ref=po_hbm.at[:, po_rows], dst_ref=p0, send_sem=psend, recv_sem=precv,
        device_id={"pipe": 1}, device_id_type=MESH,
    )

    def to_left(i):
        return pltpu.make_async_remote_copy(
            src_ref=held.at[i], dst_ref=held.at[i], send_sem=send_l.at[i], recv_sem=recv.at[i],
            device_id={"tensor": z - 1}, device_id_type=MESH,
        )

    def to_right(i):
        return pltpu.make_async_remote_copy(
            src_ref=held.at[i], dst_ref=held.at[i], send_sem=send_r.at[i], recv_sem=recv.at[i],
            device_id={"tensor": z + 1}, device_id_type=MESH,
        )

    def own_copy(q):
        return pltpu.make_async_copy(
            x_hbm.at[:, pl.ds(pl.multiple_of(q * depth, depth), depth)], held.at[z * parts + q], xs.at[q]
        )

    def weight_copy(i, side):
        return pltpu.make_async_copy(
            w_hbm.at[:, pl.ds(pl.multiple_of(i * depth, depth), depth)], wbuf.at[side], ws.at[side]
        )

    def multiply(i, side):
        @pl.loop(0, tiles)
        def _(c):
            weights = wbuf[side, pl.ds(pl.multiple_of(c * tile, tile), tile), :]
            acc[c] += lax.dot_general(held[i], weights, NT, preferred_element_type=jnp.float32)

    saved_copies = (
        pltpu.make_async_copy(ss_hbm, ss, ls.at[0]),
        pltpu.make_async_copy(sm_hbm, sm, ls.at[1]),
    )

    def in_part():
        in_sum[...] = jnp.zeros_like(in_sum)

        @pl.loop(0, tiles)
        def _(c):
            cols = pl.ds(pl.multiple_of(c * tile, tile), tile)
            gated = (ss[:, cols].astype(jnp.float32) * sm[:, cols].astype(jnp.float32)).astype(jnp.bfloat16)
            in_sum[...] += lax.dot_general(pi_ref[:, cols], gated, NT, preferred_element_type=jnp.float32)

        in_own[...] = in_sum[...].astype(jnp.bfloat16)

    def low_copy(peer):
        return pltpu.make_async_remote_copy(
            src_ref=in_own, dst_ref=in_low.at[z], send_sem=in_send.at[peer], recv_sem=low_recv.at[z],
            device_id={"pipe": 1, "tensor": peer}, device_id_type=MESH,
        )

    def up_copy(peer):
        return pltpu.make_async_remote_copy(
            src_ref=in_own, dst_ref=in_up.at[z], send_sem=in_send.at[peer], recv_sem=up_recv.at[z],
            device_id={"tensor": peer}, device_id_type=MESH,
        )

    def arrived(slots, sems, s):
        pltpu.make_async_copy(slots.at[s], slots.at[s], sems.at[s]).wait()

    def halo_copy():
        return pltpu.make_async_remote_copy(
            src_ref=in_pad.at[:, :, pl.ds(seq, taps)], dst_ref=in_pad.at[:, :, pl.ds(0, taps)],
            send_sem=halo_send, recv_sem=halo_recv, device_id={"dp": y + 1}, device_id_type=MESH,
        )

    def dp_copy(peer):
        return pltpu.make_async_remote_copy(
            src_ref=red_dp.at[y], dst_ref=red_dp.at[y], send_sem=dp_send.at[peer], recv_sem=dp_recv.at[y],
            device_id={"dp": peer}, device_id_type=MESH,
        )

    def z_copy(peer):
        return pltpu.make_async_remote_copy(
            src_ref=red_z.at[z], dst_ref=red_z.at[z], send_sem=z_send.at[peer], recv_sem=z_recv.at[z],
            device_id={"tensor": peer}, device_id_type=MESH,
        )

    fin_copy = pltpu.make_async_remote_copy(
        src_ref=final, dst_ref=final, send_sem=fin_send, recv_sem=fin_recv,
        device_id={"pipe": 0}, device_id_type=MESH,
    )

    def collect():
        in_sum[...] = jnp.zeros_like(in_sum)

        @pl.loop(0, n)
        def _(s):
            arrived(in_low, low_recv, s)
            in_sum[...] += in_low[s].astype(jnp.float32)

        for m in range(micro):
            in_pad[m, :, taps:] = in_sum[:, m * seq : (m + 1) * seq]

        @pl.when(y < dps - 1)
        def _():
            halo_copy().start()

        @pl.when(y == 0)
        def _():
            in_pad[:, :, :taps] = jnp.zeros((micro, rank, taps), jnp.float32)

        in_sum[...] = jnp.zeros_like(in_sum)

        @pl.loop(0, n)
        def _(s):
            @pl.when(s != z)
            def _():
                arrived(in_up, up_recv, s)

            in_sum[...] += in_up[s].astype(jnp.float32)

        for m in range(micro):
            span = slice(m * seq, (m + 1) * seq)
            upper[m] = jnp.dot(
                in_sum[:, span], oc_ref[1, span, :], precision=high, preferred_element_type=jnp.float32
            )
            lower[m] = jnp.dot(
                in_pad[m, :, taps:], oc_ref[0, span, :], precision=high, preferred_element_type=jnp.float32
            )

    def turn():
        @pl.when(y > 0)
        def _():
            halo_copy().wait_recv()

        for m in range(micro):
            for b in range(seq // BLOCK):
                turned[m * (seq // BLOCK) + b] = lax.dot_general(
                    in_pad[m, :, b * BLOCK : (b + 1) * BLOCK + taps], back_ref[...], NT,
                    precision=high, preferred_element_type=jnp.float32,
                )

    @pl.when(jnp.logical_not(top))
    def _():
        for copy in saved_copies:
            copy.start()
        pl.semaphore_signal(barrier, inc=1, device_id={"pipe": 1}, device_id_type=MESH)
        pl.semaphore_wait(barrier, n)
        p0_copy.start()
        for copy in saved_copies:
            copy.wait()
        in_part()

        @pl.loop(0, n)
        def _(s):
            low_copy(s).start()

        p0_copy.wait_send()

        @pl.loop(0, n)
        def _(s):
            low_copy(s).wait_send()

        fin_copy.wait_recv()
        out_ref[...] = final[:, :, :rank]

    @pl.when(top)
    def _():
        for q in range(parts):
            own_copy(q).start()
        p1_copy = pltpu.make_async_copy(po_hbm.at[:, po_rows], p1, ls.at[2])

        @pl.loop(0, n)
        def _(s):
            pl.semaphore_signal(barrier, inc=1, device_id={"pipe": 0, "tensor": s}, device_id_type=MESH)

            @pl.when(s != z)
            def _():
                pl.semaphore_signal(barrier, inc=1, device_id={"tensor": s}, device_id_type=MESH)

        @pl.loop(0, dps)
        def _(s):
            @pl.when(s != y)
            def _():
                pl.semaphore_signal(barrier, inc=1, device_id={"dp": s}, device_id_type=MESH)

        pl.semaphore_wait(barrier, n + dps - 1)

        for q in range(parts):
            own_copy(q).wait()

            @pl.when(has_left)
            def _():
                to_left(z * parts + q).start()

            @pl.when(has_right)
            def _():
                to_right(z * parts + q).start()

        p1_copy.start()
        for copy in saved_copies:
            copy.start()
        z_ref[...] = jnp.zeros_like(z_ref)
        oc_ref[...] = jnp.zeros_like(oc_ref)
        acc[...] = jnp.zeros_like(acc)
        for copy in saved_copies:
            copy.wait()
        in_part()
        in_up[z] = in_own[...]

        @pl.loop(0, n)
        def _(s):
            @pl.when(s != z)
            def _():
                up_copy(s).start()

        @pl.loop(0, tiles)
        def _(c):
            cols = pl.ds(pl.multiple_of(c * tile, tile), tile)
            spec[0:2, :, cols] = jnp.dot(
                ftab_ref[...], fm_ref[:, cols], precision=lax.Precision.HIGHEST,
                preferred_element_type=jnp.float32,
            ).reshape(2, half, tile)
            for part in range(2):
                total = jnp.zeros((half, tile), jnp.float32)
                for j in range(fs_ref.shape[0]):
                    total += ftab_ref[part * half : (part + 1) * half, j : j + 1] * fs_ref[j : j + 1, cols]
                spec[2 + part, :, cols] = total

        p1_copy.wait()
        p0_copy.wait_recv()

        @pl.loop(0, parts)
        def _(q):
            i = z * parts + q
            weight_copy(i, 0).start()
            mine = pl.ds(pl.multiple_of(q * depth, depth), depth)
            oc_ref[0] += lax.dot_general(held[i], p0[:, mine], NT, preferred_element_type=jnp.float32)
            oc_ref[1] += lax.dot_general(held[i], p1[:, mine], NT, preferred_element_type=jnp.float32)
            weight_copy(i, 0).wait()
            multiply(i, 0)

        @pl.loop(1, n)
        def _(k):
            from_left, from_right = z >= k, z + k < n

            @pl.when(k == max(1, n - 2))
            def _():
                collect()

            @pl.when(k == n - 1)
            def _():
                turn()

            @pl.loop(0, parts)
            def _(q):
                i_left, i_right = (z - k) * parts + q, (z + k) * parts + q

                @pl.when(from_left)
                def _():
                    weight_copy(i_left, 0).start()

                @pl.when(from_right)
                def _():
                    weight_copy(i_right, 1).start()

                @pl.when(from_left)
                def _():
                    to_right(i_left).wait_recv()

                    @pl.when(has_right)
                    def _():
                        to_right(i_left).start()

                @pl.when(from_right)
                def _():
                    to_left(i_right).wait_recv()

                    @pl.when(has_left)
                    def _():
                        to_left(i_right).start()

                @pl.when(from_left)
                def _():
                    weight_copy(i_left, 0).wait()
                    multiply(i_left, 0)

                @pl.when(from_right)
                def _():
                    weight_copy(i_right, 1).wait()
                    multiply(i_right, 1)

        @pl.loop(0, tiles)
        def _(c):
            cols = pl.ds(pl.multiple_of(c * tile, tile), tile)
            for b in range(rows // BLOCK):
                span = slice(b * BLOCK, (b + 1) * BLOCK)
                back = acc[c, span, :].astype(jnp.bfloat16).astype(jnp.float32)
                gate_medium = (back * ss[span, cols].astype(jnp.float32)).astype(jnp.bfloat16)
                gate_short = (back * sm[span, cols].astype(jnp.float32)).astype(jnp.bfloat16)
                gm = jnp.dot(ahead_ref[...], gate_medium, preferred_element_type=jnp.float32)
                gs = jnp.dot(ahead_ref[...], gate_short, preferred_element_type=jnp.float32)
                m_re, m_im = spec[0, :, cols], spec[1, :, cols]
                s_re, s_im = spec[2, :, cols], spec[3, :, cols]
                real = m_re * gm[:half] - m_im * gm[half:] + s_re * gs[:half] - s_im * gs[half:]
                imag = m_re * gm[half:] + m_im * gm[:half] + s_re * gs[half:] + s_im * gs[:half]
                basis = p0[:, cols]
                base = 2 * half * b
                z_ref[base : base + half, :] += lax.dot_general(
                    real.astype(jnp.bfloat16), basis, NT, preferred_element_type=jnp.float32
                )
                z_ref[base + half : base + 2 * half, :] += lax.dot_general(
                    imag.astype(jnp.bfloat16), basis, NT, preferred_element_type=jnp.float32
                )

        size = 2 * half
        for m in range(micro):
            total = lower[m]
            for b in range(seq // BLOCK):
                at = m * (seq // BLOCK) + b
                total += jnp.dot(
                    turned[at], z_ref[at * size : (at + 1) * size, :], precision=high,
                    preferred_element_type=jnp.float32,
                )
            red_dp[y, m] = jnp.concatenate([total, upper[m]], axis=1) * scale

        @pl.loop(0, dps)
        def _(s):
            @pl.when(s != y)
            def _():
                dp_copy(s).start()

        @pl.loop(0, dps)
        def _(s):
            @pl.when(s != y)
            def _():
                arrived(red_dp, dp_recv, s)

        total = red_dp[0]
        for s in range(1, dps):
            total += red_dp[s]
        red_z[z] = total

        @pl.loop(0, n)
        def _(s):
            @pl.when(s != z)
            def _():
                z_copy(s).start()

        @pl.loop(0, n)
        def _(s):
            @pl.when(s != z)
            def _():
                arrived(red_z, z_recv, s)

        total = red_z[0]
        for s in range(1, n):
            total += red_z[s]
        final[...] = total
        fin_copy.start()
        out_ref[...] = final[:, :, rank:]
        fin_copy.wait_send()

        @pl.when(y < dps - 1)
        def _():
            halo_copy().wait_send()

        @pl.loop(0, dps)
        def _(s):
            @pl.when(s != y)
            def _():
                dp_copy(s).wait_send()

        @pl.loop(0, n)
        def _(s):
            @pl.when(s != z)
            def _():
                z_copy(s).wait_send()
                up_copy(s).wait_send()

            @pl.loop(0, parts)
            def _(q):
                i = s * parts + q

                @pl.when(jnp.logical_and(has_left, s >= z))
                def _():
                    to_left(i).wait_send()

                @pl.when(jnp.logical_and(has_right, s <= z))
                def _():
                    to_right(i).wait_send()


def body(
    cotangent, saved_short, saved_medium, out_weight, short_filter, medium_filter, proj_in, proj_out
):
    n, dps = lax.axis_size("tensor"), lax.axis_size("dp")
    micro, seq, width = cotangent.shape
    rows = micro * seq
    channels = saved_short.shape[3]
    rank = proj_in.shape[2]
    taps = medium_filter.shape[1]
    ahead, ftab, back = transforms(taps)
    size = ahead.shape[0]
    depth = min(512, width)
    parts = width // depth
    tile = min(256, channels)
    blocks = rows // BLOCK
    any_spec = pl.BlockSpec(memory_space=pl.ANY)
    vmem = pl.BlockSpec(memory_space=pltpu.VMEM)
    dma = pltpu.SemaphoreType.DMA
    low, full = jnp.bfloat16, jnp.float32
    grads = pl.pallas_call(
        functools.partial(kernel, n, parts, tile),
        out_shape=jax.ShapeDtypeStruct((micro, rank, rank), full),
        in_specs=[any_spec] * 5 + [vmem] * 6,
        out_specs=vmem,
        scratch_shapes=[
            pltpu.VMEM((n * parts, rows, depth), low),
            pltpu.VMEM((channels // tile, rows, tile), full),
            pltpu.VMEM((2, channels, depth), low),
            pltpu.VMEM((rows, channels), low),
            pltpu.VMEM((rows, channels), low),
            pltpu.VMEM((rank, width), low),
            pltpu.VMEM((rank, width), low),
            pltpu.VMEM((4, size // 2, channels), full),
            pltpu.VMEM((blocks * size, rank), full),
            pltpu.VMEM((2, rows, rank), full),
            pltpu.VMEM((rank, rows), low),
            pltpu.VMEM((rank, rows), full),
            pltpu.VMEM((n, rank, rows), low),
            pltpu.VMEM((n, rank, rows), low),
            pltpu.VMEM((micro, rank, taps + seq), full),
            pltpu.VMEM((blocks, rank, size), full),
            pltpu.VMEM((micro, rank, rank), full),
            pltpu.VMEM((micro, rank, rank), full),
            pltpu.VMEM((dps, micro, rank, 2 * rank), full),
            pltpu.VMEM((n, micro, rank, 2 * rank), full),
            pltpu.VMEM((micro, rank, 2 * rank), full),
            dma((parts,)), dma((2,)), dma((3,)),
            dma((n * parts,)), dma((n * parts,)), dma((n * parts,)),
            dma, dma,
            dma((n,)), dma((n,)), dma((n,)), dma, dma,
            dma((dps,)), dma((dps,)), dma((n,)), dma((n,)), dma, dma,
        ],
        cost_estimate=pl.CostEstimate(
            flops=2 * rows * channels * width * n, bytes_accessed=2 * channels * width * n, transcendentals=0
        ),
        compiler_params=pltpu.CompilerParams(
            collective_id=0, has_side_effects=True, vmem_limit_bytes=60 * 2**20
        ),
        name="back_pass",
    )(
        cotangent.reshape(rows, width), out_weight[0], saved_short.reshape(rows, channels),
        saved_medium.reshape(rows, channels), proj_out[0].T, proj_in[0].T,
        medium_filter[0], short_filter[0], jnp.asarray(ahead), jnp.asarray(ftab), jnp.asarray(back),
    )
    return grads[None]


def solution(mesh):
    in_specs = (
        P(None, "dp", "tensor"),
        P("pipe", None, "dp", "tensor"),
        P("pipe", None, "dp", "tensor"),
        P("pipe", "tensor", None),
        P("pipe", None, "tensor"),
        P("pipe", None, "tensor"),
        P("pipe", "tensor", None),
        P("pipe", None, None),
    )
    out_specs = P("pipe", None, None, None)
    return jax.shard_map(body, mesh=mesh, in_specs=in_specs, out_specs=out_specs, check_vma=False)
```

time: 348 us -> 180 us (0.52)
  Pallas kernels: 5.06 us -> 176 us
  waiting for transfers between devices: 157 us -> 0 us
  starting transfers between devices: 156 us -> 0 us
  between operations: 13.6 us -> 0.01 us
  other arithmetic: 6.12 us -> 0 us
  local copies, waits for them, and re-layouts: 6.81 us -> 2.94 us
  matrix products: 3.79 us -> 0 us
    pallas_call x1, Pallas kernels: 5.06 us -> 176 us  [body(): pl.pallas_call(functools.partial(kernel, n, parts, tile), out_shape=jax.S...]
    psum x2 -> x0, waiting for transfers between devices: 156 us -> none  [the longest x1 121 us: body(): lax.psum(jnp.stack([lower, upper]) * norm_factor, ('pipe', 'tensor', 'dp'))]
    ppermute x2 -> x0, starting transfers between devices: 156 us -> none  [passed_along(): return lax.ppermute(array, axis, pairs)]
    convert_element_type x1 -> x0, other arithmetic: 5.42 us -> none  [body(): (ss.astype(jnp.float32) * sm.astype(jnp.float32)).astype(jnp.bfloat16)]
    dot_general x5 -> x0, matrix products: 3.79 us -> none  [the longest x1 1.4 us: body(): in_part = jnp.dot(gated, proj_in[0], preferred_element_type=jnp.float32)]
  transfers between devices with their start and end apart: 4 -> 0, of which waited for: 2 -> 0; matrix products, arithmetic and copies ran while one was open for 1% -> 0% of each run, Pallas kernels for 1% -> 0%
where the time goes in v2:
time: 180 us; the launch traced here: 179 us
  Pallas kernels  176 us (98%)
  local copies, waits for them, and re-layouts  2.94 us (2%)
    pallas_call x1, Pallas kernels, body(): pl.pallas_call(functools.partial(kernel, n, parts, tile), out_shape=jax.S...  176 us

profile of v2, /device:TPU:0, one launch (start us, length us, event | category | flops | bytes accessed | tf_op | source)
XLA Modules:
  0.0 179.3 jit_solution(10009914155886615481)
XLA Ops:
  0.0 1.5 copy.14
  1.5 176.4 %back_pass.1 = f32[2,64,64]{2,1,0:T(8,128)} custom-call(bf16[1024,2048]{1,0:T(8,128)(2,1)} %bitcast.18, bf16[2048,8192]{1,0:T(8,128)(2,1)} %bitcast.17, bf16[1024,2048]{1,0:T(8,128)(2,1)} %bitcast.19, bf16[1024,2048]{1,0:T(8,128)(2,1)} %bitcast.20, bf16[64,8192]{1,0:T(8,128)(2,1)} %bitcast.21, bf16[64,2048]{1,0:T(8,128)(2,1)} %bitcast.23, ...), custom_call_target="tpu_custom_call" | custom-call | flops 34359738368 | bytes 33554432 | tf_op jit(solution)/shard_map/back_pass/pallas_call | solution.py:465
  177.8 1.5 copy.16

commit v3 on v2

v3 whole, which is shorter than its diff:
```python
import functools
import math

import jax
import jax.numpy as jnp
import numpy as np
from jax import lax
from jax.experimental import pallas as pl
from jax.experimental.pallas import tpu as pltpu
from jax.sharding import PartitionSpec as P

MESH = pl.DeviceIdType.MESH
BLOCK = 256
NT = (((1,), (1,)), ((), ()))


def transforms(taps):
    size = BLOCK + taps
    freq = 2.0 * np.pi * (np.arange(size // 2) + 0.5) / size

    def table(times, sign):
        angle = freq[:, None] * times[None, :]
        return np.concatenate([np.cos(angle), sign * np.sin(angle)], axis=0)

    ahead = table(np.arange(BLOCK), -1.0).astype(jnp.bfloat16)
    filters = table(np.arange(taps), 1.0).astype(np.float32)
    back = (table(np.arange(-taps, BLOCK), -1.0) * (2.0 / size)).astype(np.float32)
    return ahead, filters, back


def kernel(
    n, tile,
    x_hbm, w_hbm, ss_hbm, sm_hbm, po_hbm, pi_ref, fm_ref, fs_ref, ahead_ref, ftab_ref, back_ref,
    out_ref,
    held, acc, wbuf, ss, sm, p0, p1, spec, z_ref, oc_ref,
    in_own, in_sum, in_low, in_up, in_pad, turned, lower, upper, red_dp, red_z, final,
    xs, ws, ls, send_l, send_r, recv, psend, precv,
    in_send, low_recv, halo_send, halo_recv,
    dp_send, dp_recv, z_send, z_recv, fin_send, fin_recv,
):
    z = lax.axis_index("tensor")
    y = lax.axis_index("dp")
    dps = red_dp.shape[0]
    micro, rank, padded = in_pad.shape
    parts, width = held.shape[1], held.shape[3]
    taps = padded - parts * BLOCK // micro
    seq = padded - taps
    scale = 1.0 / math.sqrt(seq * dps)
    high = lax.Precision.HIGHEST
    top = lax.axis_index("pipe") == lax.axis_size("pipe") - 1
    has_left, has_right = z > 0, z < n - 1
    half = spec.shape[1]
    tiles = spec.shape[2] // tile
    barrier = pltpu.get_barrier_semaphore()
    po_rows = pl.ds(pl.multiple_of(z * width, width), width)

    p0_copy = pltpu.make_async_remote_copy(
        src_ref=po_hbm.at[:, po_rows], dst_ref=p0, send_sem=psend, recv_sem=precv,
        device_id={"pipe": 1}, device_id_type=MESH,
    )

    def to_left(s, r, src=None):
        return pltpu.make_async_remote_copy(
            src_ref=held.at[s, r] if src is None else src, dst_ref=held.at[s, r],
            send_sem=send_l.at[s, r], recv_sem=recv.at[s, r],
            device_id={"tensor": z - 1}, device_id_type=MESH,
        )

    def to_right(s, r, src=None):
        return pltpu.make_async_remote_copy(
            src_ref=held.at[s, r] if src is None else src, dst_ref=held.at[s, r],
            send_sem=send_r.at[s, r], recv_sem=recv.at[s, r],
            device_id={"tensor": z + 1}, device_id_type=MESH,
        )

    def own_rows(r):
        return x_hbm.at[pl.ds(r * BLOCK, BLOCK), :]

    def own_copy(r):
        return pltpu.make_async_copy(own_rows(r), held.at[z, r], xs.at[r])

    def weight_copy(s):
        return pltpu.make_async_copy(
            w_hbm.at[:, pl.ds(pl.multiple_of(s * width, width), width)], wbuf, ws
        )

    def shard_cols(s):
        return pl.ds(pl.multiple_of(s * width, width), width)

    def multiply(s):
        weight_copy(s).start()
        shard = held[s].reshape(parts * BLOCK, width)
        oc_ref[1] += lax.dot_general(
            shard, p1[:, shard_cols(s)], NT, preferred_element_type=jnp.float32
        ).reshape(parts, BLOCK, rank)
        weight_copy(s).wait()

        @pl.loop(0, tiles)
        def _(c):
            weights = wbuf[pl.ds(pl.multiple_of(c * tile, tile), tile), :]
            acc[c] += lax.dot_general(
                held[s].reshape(parts * BLOCK, width), weights, NT, preferred_element_type=jnp.float32
            ).reshape(parts, BLOCK, tile)

    saved_copies = (
        pltpu.make_async_copy(ss_hbm, ss, ls.at[0]),
        pltpu.make_async_copy(sm_hbm, sm, ls.at[1]),
    )

    def in_part():
        in_sum[...] = jnp.zeros_like(in_sum)

        @pl.loop(0, tiles)
        def _(c):
            cols = pl.ds(pl.multiple_of(c * tile, tile), tile)
            gated = (ss[:, cols].astype(jnp.float32) * sm[:, cols].astype(jnp.float32)).astype(jnp.bfloat16)
            in_sum[...] += lax.dot_general(pi_ref[:, cols], gated, NT, preferred_element_type=jnp.float32)

    def low_copy(peer):
        return pltpu.make_async_remote_copy(
            src_ref=in_own, dst_ref=in_low.at[z], send_sem=in_send.at[peer], recv_sem=low_recv.at[z],
            device_id={"pipe": 1, "tensor": peer}, device_id_type=MESH,
        )

    def arrived(slots, sems, s):
        pltpu.make_async_copy(slots.at[s], slots.at[s], sems.at[s]).wait()

    def halo_copy():
        return pltpu.make_async_remote_copy(
            src_ref=in_pad.at[:, :, pl.ds(seq, taps)], dst_ref=in_pad.at[:, :, pl.ds(0, taps)],
            send_sem=halo_send, recv_sem=halo_recv, device_id={"dp": y + 1}, device_id_type=MESH,
        )

    def dp_copy(peer):
        return pltpu.make_async_remote_copy(
            src_ref=red_dp.at[y], dst_ref=red_dp.at[y], send_sem=dp_send.at[peer], recv_sem=dp_recv.at[y],
            device_id={"dp": peer}, device_id_type=MESH,
        )

    def z_copy(peer):
        return pltpu.make_async_remote_copy(
            src_ref=red_z.at[z], dst_ref=red_z.at[z], send_sem=z_send.at[peer], recv_sem=z_recv.at[z],
            device_id={"tensor": peer}, device_id_type=MESH,
        )

    fin_copy = pltpu.make_async_remote_copy(
        src_ref=final, dst_ref=final, send_sem=fin_send, recv_sem=fin_recv,
        device_id={"pipe": 0}, device_id_type=MESH,
    )

    def collect():
        in_sum[...] = jnp.zeros_like(in_sum)

        @pl.loop(0, n)
        def _(s):
            arrived(in_low, low_recv, s)
            in_sum[...] += in_low[s].astype(jnp.float32)

        for m in range(micro):
            in_pad[m, :, taps:] = in_sum[:, m * seq : (m + 1) * seq]

        @pl.when(y < dps - 1)
        def _():
            halo_copy().start()

        @pl.when(y == 0)
        def _():
            in_pad[:, :, :taps] = jnp.zeros((micro, rank, taps), jnp.float32)

        for m in range(micro):
            each = parts // micro
            lower[m] = jnp.dot(
                in_pad[m, :, taps:], oc_ref[0, m * each : (m + 1) * each].reshape(seq, rank),
                precision=high, preferred_element_type=jnp.float32,
            )

    def turn():
        @pl.when(y > 0)
        def _():
            halo_copy().wait_recv()

        for m in range(micro):
            for b in range(seq // BLOCK):
                turned[m * (seq // BLOCK) + b] = lax.dot_general(
                    in_pad[m, :, b * BLOCK : (b + 1) * BLOCK + taps], back_ref[...], NT,
                    precision=high, preferred_element_type=jnp.float32,
                )

    @pl.when(jnp.logical_not(top))
    def _():
        for copy in saved_copies:
            copy.start()
        pl.semaphore_signal(barrier, inc=1, device_id={"pipe": 1}, device_id_type=MESH)
        pl.semaphore_wait(barrier, n)
        p0_copy.start()
        for copy in saved_copies:
            copy.wait()
        in_part()
        in_own[...] = in_sum[...].astype(jnp.bfloat16)

        @pl.loop(0, n)
        def _(s):
            low_copy(s).start()

        p0_copy.wait_send()

        @pl.loop(0, n)
        def _(s):
            low_copy(s).wait_send()

        fin_copy.wait_recv()
        out_ref[...] = final[:, :, :rank]

    @pl.when(top)
    def _():
        for r in range(parts):
            own_copy(r).start()
        p1_copy = pltpu.make_async_copy(po_hbm, p1, ls.at[2])

        @pl.loop(0, n)
        def _(s):
            pl.semaphore_signal(barrier, inc=1, device_id={"pipe": 0, "tensor": s}, device_id_type=MESH)

            @pl.when(s != z)
            def _():
                pl.semaphore_signal(barrier, inc=1, device_id={"tensor": s}, device_id_type=MESH)

        @pl.loop(0, dps)
        def _(s):
            @pl.when(s != y)
            def _():
                pl.semaphore_signal(barrier, inc=1, device_id={"dp": s}, device_id_type=MESH)

        pl.semaphore_wait(barrier, n + dps - 1)

        for r in range(parts):
            @pl.when(has_left)
            def _():
                to_left(z, r, own_rows(r)).start()

            @pl.when(has_right)
            def _():
                to_right(z, r, own_rows(r)).start()

        p1_copy.start()
        for copy in saved_copies:
            copy.start()
        oc_ref[...] = jnp.zeros_like(oc_ref)
        upper[...] = jnp.zeros_like(upper)
        acc[...] = jnp.zeros_like(acc)
        for copy in saved_copies:
            copy.wait()
        in_part()
        in_up[...] = in_sum[...]

        @pl.loop(0, tiles)
        def _(c):
            cols = pl.ds(pl.multiple_of(c * tile, tile), tile)
            spec[0:2, :, cols] = jnp.dot(
                ftab_ref[...], fm_ref[:, cols], precision=lax.Precision.HIGHEST,
                preferred_element_type=jnp.float32,
            ).reshape(2, half, tile)
            for part in range(2):
                total = jnp.zeros((half, tile), jnp.float32)
                for j in range(fs_ref.shape[0]):
                    total += ftab_ref[part * half : (part + 1) * half, j : j + 1] * fs_ref[j, :, cols]
                spec[2 + part, :, cols] = total

        p1_copy.wait()
        p0_copy.wait_recv()
        for r in range(parts):
            own_copy(r).wait()
        oc_ref[0] = lax.dot_general(
            held[z].reshape(parts * BLOCK, width), p0[...], NT, preferred_element_type=jnp.float32
        ).reshape(parts, BLOCK, rank)
        multiply(z)
        if n < 3:
            collect()

        @pl.loop(1, n - 1)
        def _(k):
            from_left, from_right = z >= k, z + k < n

            @pl.when(k == n - 2)
            def _():
                collect()

            @pl.loop(0, parts)
            def _(r):
                @pl.when(from_left)
                def _():
                    to_right(z - k, r).wait_recv()

                    @pl.when(has_right)
                    def _():
                        to_right(z - k, r).start()

                @pl.when(from_right)
                def _():
                    to_left(z + k, r).wait_recv()

                    @pl.when(has_left)
                    def _():
                        to_left(z + k, r).start()

            @pl.when(from_left)
            def _():
                multiply(z - k)

            @pl.when(from_right)
            def _():
                multiply(z + k)

        is_end = jnp.logical_or(z == 0, z == n - 1)
        farthest = n - 1 - z

        @pl.when(is_end)
        def _():
            weight_copy(farthest).start()

        turn()

        @pl.when(is_end)
        def _():
            weight_copy(farthest).wait()

        each = parts // micro

        @pl.loop(0, parts)
        def _(r):
            @pl.when(is_end)
            def _():
                to_left(farthest, r).wait_recv()
                oc_ref[1, r] += lax.dot_general(
                    held[farthest, r], p1[:, shard_cols(farthest)], NT, preferred_element_type=jnp.float32
                )

            z_ref[...] = jnp.zeros_like(z_ref)
            span = pl.ds(pl.multiple_of(r * BLOCK, BLOCK), BLOCK)

            @pl.loop(0, tiles)
            def _(c):
                cols = pl.ds(pl.multiple_of(c * tile, tile), tile)

                @pl.when(is_end)
                def _():
                    acc[c, r] += lax.dot_general(
                        held[farthest, r], wbuf[cols, :], NT, preferred_element_type=jnp.float32
                    )

                back = acc[c, r].astype(jnp.bfloat16).astype(jnp.float32)
                gate_medium = (back * ss[span, cols].astype(jnp.float32)).astype(jnp.bfloat16)
                gate_short = (back * sm[span, cols].astype(jnp.float32)).astype(jnp.bfloat16)
                gm = jnp.dot(ahead_ref[...], gate_medium, preferred_element_type=jnp.float32)
                gs = jnp.dot(ahead_ref[...], gate_short, preferred_element_type=jnp.float32)
                m_re, m_im = spec[0, :, cols], spec[1, :, cols]
                s_re, s_im = spec[2, :, cols], spec[3, :, cols]
                real = m_re * gm[:half] - m_im * gm[half:] + s_re * gs[:half] - s_im * gs[half:]
                imag = m_re * gm[half:] + m_im * gm[:half] + s_re * gs[half:] + s_im * gs[:half]
                both = jnp.concatenate([real, imag], axis=0).astype(jnp.bfloat16)
                z_ref[...] += lax.dot_general(both, p0[:, cols], NT, preferred_element_type=jnp.float32)

            m = r // each
            lower[m] += jnp.dot(
                turned[r], z_ref[...], precision=high, preferred_element_type=jnp.float32
            )
            upper[m] += jnp.dot(
                in_up[:, span], oc_ref[1, r], precision=high, preferred_element_type=jnp.float32
            )

        for m in range(micro):
            red_dp[y, m] = jnp.concatenate([lower[m], upper[m]], axis=1) * scale

        @pl.loop(0, dps)
        def _(s):
            @pl.when(s != y)
            def _():
                dp_copy(s).start()

        @pl.loop(0, dps)
        def _(s):
            @pl.when(s != y)
            def _():
                arrived(red_dp, dp_recv, s)

        total = red_dp[0]
        for s in range(1, dps):
            total += red_dp[s]
        red_z[z] = total

        @pl.loop(0, n)
        def _(s):
            @pl.when(s != z)
            def _():
                z_copy(s).start()

        @pl.loop(0, n)
        def _(s):
            @pl.when(s != z)
            def _():
                arrived(red_z, z_recv, s)

        total = red_z[0]
        for s in range(1, n):
            total += red_z[s]
        final[...] = total
        fin_copy.start()
        out_ref[...] = final[:, :, rank:]
        fin_copy.wait_send()

        @pl.when(y < dps - 1)
        def _():
            halo_copy().wait_send()

        @pl.loop(0, dps)
        def _(s):
            @pl.when(s != y)
            def _():
                dp_copy(s).wait_send()

        @pl.loop(0, n)
        def _(s):
            @pl.when(s != z)
            def _():
                z_copy(s).wait_send()

            @pl.loop(0, parts)
            def _(r):
                @pl.when(jnp.logical_and(has_left, s >= z))
                def _():
                    to_left(s, r).wait_send()

                @pl.when(jnp.logical_and(has_right, s <= z))
                def _():
                    to_right(s, r).wait_send()


def body(
    cotangent, saved_short, saved_medium, out_weight, short_filter, medium_filter, proj_in, proj_out
):
    n, dps = lax.axis_size("tensor"), lax.axis_size("dp")
    micro, seq, width = cotangent.shape
    rows = micro * seq
    channels = saved_short.shape[3]
    rank = proj_in.shape[2]
    taps = medium_filter.shape[1]
    ahead, ftab, back = transforms(taps)
    size = ahead.shape[0]
    tile = min(256, channels)
    parts = rows // BLOCK
    any_spec = pl.BlockSpec(memory_space=pl.ANY)
    vmem = pl.BlockSpec(memory_space=pltpu.VMEM)
    dma = pltpu.SemaphoreType.DMA
    low, full = jnp.bfloat16, jnp.float32
    grads = pl.pallas_call(
        functools.partial(kernel, n, tile),
        out_shape=jax.ShapeDtypeStruct((micro, rank, rank), full),
        in_specs=[any_spec] * 5 + [vmem] * 6,
        out_specs=vmem,
        scratch_shapes=[
            pltpu.VMEM((n, parts, BLOCK, width), low),
            pltpu.VMEM((channels // tile, parts, BLOCK, tile), full),
            pltpu.VMEM((channels, width), low),
            pltpu.VMEM((rows, channels), low),
            pltpu.VMEM((rows, channels), low),
            pltpu.VMEM((rank, width), low),
            pltpu.VMEM((rank, n * width), low),
            pltpu.VMEM((4, size // 2, channels), full),
            pltpu.VMEM((size, rank), full),
            pltpu.VMEM((2, parts, BLOCK, rank), full),
            pltpu.VMEM((rank, rows), low),
            pltpu.VMEM((rank, rows), full),
            pltpu.VMEM((n, rank, rows), low),
            pltpu.VMEM((rank, rows), full),
            pltpu.VMEM((micro, rank, taps + seq), full),
            pltpu.VMEM((parts, rank, size), full),
            pltpu.VMEM((micro, rank, rank), full),
            pltpu.VMEM((micro, rank, rank), full),
            pltpu.VMEM((dps, micro, rank, 2 * rank), full),
            pltpu.VMEM((n, micro, rank, 2 * rank), full),
            pltpu.VMEM((micro, rank, 2 * rank), full),
            dma((parts,)), dma, dma((3,)),
            dma((n, parts)), dma((n, parts)), dma((n, parts)),
            dma, dma,
            dma((n,)), dma((n,)), dma, dma,
            dma((dps,)), dma((dps,)), dma((n,)), dma((n,)), dma, dma,
        ],
        cost_estimate=pl.CostEstimate(
            flops=2 * rows * channels * width * n, bytes_accessed=2 * channels * width * n, transcendentals=0
        ),
        compiler_params=pltpu.CompilerParams(
            collective_id=0, has_side_effects=True, vmem_limit_bytes=60 * 2**20
        ),
        name="back_pass",
    )(
        cotangent.reshape(rows, width), out_weight[0], saved_short.reshape(rows, channels),
        saved_medium.reshape(rows, channels), proj_out[0].T, proj_in[0].T,
        medium_filter[0], short_filter.transpose(1, 0, 2), jnp.asarray(ahead), jnp.asarray(ftab), jnp.asarray(back),
    )
    return grads[None]


def solution(mesh):
    in_specs = (
        P(None, "dp", "tensor"),
        P("pipe", None, "dp", "tensor"),
        P("pipe", None, "dp", "tensor"),
        P("pipe", "tensor", None),
        P("pipe", None, "tensor"),
        P("pipe", None, "tensor"),
        P("pipe", "tensor", None),
        P("pipe", None, None),
    )
    out_specs = P("pipe", None, None, None)
    return jax.shard_map(body, mesh=mesh, in_specs=in_specs, out_specs=out_specs, check_vma=False)
```

time: 180 us -> 167 us (0.928)
  Pallas kernels: 176 us -> 165 us
    pallas_call x1, Pallas kernels: 176 us -> 165 us  [body(): pl.pallas_call(functools.partial(kernel, n, tile), out_shape=jax.ShapeDty...]
where the time goes in v3:
time: 167 us; the launch traced here: 166 us
  Pallas kernels  165 us (99%)
    pallas_call x1, Pallas kernels, body(): pl.pallas_call(functools.partial(kernel, n, tile), out_shape=jax.ShapeDty...  165 us

profile of v3, /device:TPU:0, one launch (start us, length us, event | category | flops | bytes accessed | tf_op | source)
XLA Modules:
  0.0 166.5 jit_solution(16081377628299212235)
XLA Ops:
  0.0 165.0 %back_pass.1 = f32[2,64,64]{2,1,0:T(8,128)} custom-call(bf16[1024,2048]{1,0:T(8,128)(2,1)} %bitcast.15, bf16[2048,8192]{1,0:T(8,128)(2,1)} %bitcast.14, bf16[1024,2048]{1,0:T(8,128)(2,1)} %bitcast.16, bf16[1024,2048]{1,0:T(8,128)(2,1)} %bitcast.17, bf16[64,8192]{1,0:T(8,128)(2,1)} %bitcast.18, bf16[64,2048]{1,0:T(8,128)(2,1)} %bitcast.20, ...), custom_call_target="tpu_custom_call" | custom-call | flops 34359738368 | bytes 33554432 | tf_op jit(solution)/shard_map/back_pass/pallas_call | solution.py:455
  165.0 1.5 copy.13

commit v4 on v3

--- a/solution.py
+++ b/solution.py
@@ -11,6 +11,7 @@
 
 MESH = pl.DeviceIdType.MESH
 BLOCK = 256
+HALF = BLOCK // 2
 NT = (((1,), (1,)), ((), ()))
 
 
@@ -59,25 +60,30 @@
         device_id={"pipe": 1}, device_id_type=MESH,
     )
 
-    def to_left(s, r, src=None):
+    pieces = 2 * parts
+
+    def piece(s, g):
+        return held.at[s, g // 2, pl.ds(pl.multiple_of((g % 2) * HALF, HALF), HALF), :]
+
+    def to_left(s, g, src=None):
         return pltpu.make_async_remote_copy(
-            src_ref=held.at[s, r] if src is None else src, dst_ref=held.at[s, r],
-            send_sem=send_l.at[s, r], recv_sem=recv.at[s, r],
+            src_ref=piece(s, g) if src is None else src, dst_ref=piece(s, g),
+            send_sem=send_l.at[s, g], recv_sem=recv.at[s, g],
             device_id={"tensor": z - 1}, device_id_type=MESH,
         )
 
-    def to_right(s, r, src=None):
+    def to_right(s, g, src=None):
         return pltpu.make_async_remote_copy(
-            src_ref=held.at[s, r] if src is None else src, dst_ref=held.at[s, r],
-            send_sem=send_r.at[s, r], recv_sem=recv.at[s, r],
+            src_ref=piece(s, g) if src is None else src, dst_ref=piece(s, g),
+            send_sem=send_r.at[s, g], recv_sem=recv.at[s, g],
             device_id={"tensor": z + 1}, device_id_type=MESH,
         )
 
-    def own_rows(r):
-        return x_hbm.at[pl.ds(r * BLOCK, BLOCK), :]
+    def own_piece(g):
+        return x_hbm.at[pl.ds(g * HALF, HALF), :]
 
     def own_copy(r):
-        return pltpu.make_async_copy(own_rows(r), held.at[z, r], xs.at[r])
+        return pltpu.make_async_copy(x_hbm.at[pl.ds(r * BLOCK, BLOCK), :], held.at[z, r], xs.at[r])
 
     def weight_copy(s):
         return pltpu.make_async_copy(
@@ -233,14 +239,14 @@
 
         pl.semaphore_wait(barrier, n + dps - 1)
 
-        for r in range(parts):
+        for g in range(pieces):
             @pl.when(has_left)
             def _():
-                to_left(z, r, own_rows(r)).start()
+                to_left(z, g, own_piece(g)).start()
 
             @pl.when(has_right)
             def _():
-                to_right(z, r, own_rows(r)).start()
+                to_right(z, g, own_piece(g)).start()
 
         p1_copy.start()
         for copy in saved_copies:
@@ -285,23 +291,27 @@
             def _():
                 collect()
 
-            @pl.loop(0, parts)
-            def _(r):
+            in_order = k == n - 2
+
+            @pl.loop(0, pieces)
+            def _(g):
+                at_once = jnp.logical_or(jnp.logical_not(in_order), g < 2)
+
                 @pl.when(from_left)
                 def _():
-                    to_right(z - k, r).wait_recv()
-
-                    @pl.when(has_right)
+                    to_right(z - k, g).wait_recv()
+
+                    @pl.when(jnp.logical_and(has_right, at_once))
                     def _():
-                        to_right(z - k, r).start()
+                        to_right(z - k, g).start()
 
                 @pl.when(from_right)
                 def _():
-                    to_left(z + k, r).wait_recv()
-
-                    @pl.when(has_left)
+                    to_left(z + k, g).wait_recv()
+
+                    @pl.when(jnp.logical_and(has_left, at_once))
                     def _():
-                        to_left(z + k, r).start()
+                        to_left(z + k, g).start()
 
             @pl.when(from_left)
             def _():
@@ -310,6 +320,20 @@
             @pl.when(from_right)
             def _():
                 multiply(z + k)
+
+            @pl.when(in_order)
+            def _():
+                @pl.loop(2, pieces)
+                def _(g):
+                    @pl.when(jnp.logical_and(from_left, has_right))
+                    def _():
+                        to_right(z - k, g - 2).wait_send()
+                        to_right(z - k, g).start()
+
+                    @pl.when(jnp.logical_and(from_right, has_left))
+                    def _():
+                        to_left(z + k, g - 2).wait_send()
+                        to_left(z + k, g).start()
 
         is_end = jnp.logical_or(z == 0, z == n - 1)
         farthest = n - 1 - z
@@ -330,7 +354,8 @@
         def _(r):
             @pl.when(is_end)
             def _():
-                to_left(farthest, r).wait_recv()
+                to_left(farthest, 2 * r).wait_recv()
+                to_left(farthest, 2 * r + 1).wait_recv()
                 oc_ref[1, r] += lax.dot_general(
                     held[farthest, r], p1[:, shard_cols(farthest)], NT, preferred_element_type=jnp.float32
                 )
@@ -424,15 +449,21 @@
             def _():
                 z_copy(s).wait_send()
 
-            @pl.loop(0, parts)
-            def _(r):
-                @pl.when(jnp.logical_and(has_left, s >= z))
+            @pl.loop(0, pieces)
+            def _(g):
+                left = jnp.logical_and(has_left, s >= z)
+                right = jnp.logical_and(has_right, s <= z)
+                if n > 2:
+                    left = jnp.logical_and(left, jnp.logical_or(s - z != n - 2, g >= pieces - 2))
+                    right = jnp.logical_and(right, jnp.logical_or(z - s != n - 2, g >= pieces - 2))
+
+                @pl.when(left)
                 def _():
-                    to_left(s, r).wait_send()
-
-                @pl.when(jnp.logical_and(has_right, s <= z))
+                    to_left(s, g).wait_send()
+
+                @pl.when(right)
                 def _():
-                    to_right(s, r).wait_send()
+                    to_right(s, g).wait_send()
 
 
 def body(
@@ -480,7 +511,7 @@
             pltpu.VMEM((n, micro, rank, 2 * rank), full),
             pltpu.VMEM((micro, rank, 2 * rank), full),
             dma((parts,)), dma, dma((3,)),
-            dma((n, parts)), dma((n, parts)), dma((n, parts)),
+            dma((n, 2 * parts)), dma((n, 2 * parts)), dma((n, 2 * parts)),
             dma, dma,
             dma((n,)), dma((n,)), dma, dma,
             dma((dps,)), dma((dps,)), dma((n,)), dma((n,)), dma, dma,

time: 167 us -> 173 us (1.036)
  Pallas kernels: 165 us -> 171 us
    pallas_call x1, Pallas kernels: 165 us -> 171 us  [body(): pl.pallas_call(functools.partial(kernel, n, tile), out_shape=jax.ShapeDty...]
where the time goes in v4:
time: 173 us; the launch traced here: 172 us
  Pallas kernels  171 us (99%)
    pallas_call x1, Pallas kernels, body(): pl.pallas_call(functools.partial(kernel, n, tile), out_shape=jax.ShapeDty...  171 us

profile of v4, /device:TPU:0, one launch (start us, length us, event | category | flops | bytes accessed | tf_op | source)
XLA Modules:
  0.0 172.3 jit_solution(13977638072503215222)
XLA Ops:
  0.0 170.9 %back_pass.1 = f32[2,64,64]{2,1,0:T(8,128)} custom-call(bf16[1024,2048]{1,0:T(8,128)(2,1)} %bitcast.15, bf16[2048,8192]{1,0:T(8,128)(2,1)} %bitcast.14, bf16[1024,2048]{1,0:T(8,128)(2,1)} %bitcast.16, bf16[1024,2048]{1,0:T(8,128)(2,1)} %bitcast.17, bf16[64,8192]{1,0:T(8,128)(2,1)} %bitcast.18, bf16[64,2048]{1,0:T(8,128)(2,1)} %bitcast.20, ...), custom_call_target="tpu_custom_call" | custom-call | flops 34359738368 | bytes 33554432 | tf_op jit(solution)/shard_map/back_pass/pallas_call | solution.py:486
  170.9 1.5 copy.13

commit v5 on v3

--- a/solution.py
+++ b/solution.py
@@ -33,7 +33,7 @@
     x_hbm, w_hbm, ss_hbm, sm_hbm, po_hbm, pi_ref, fm_ref, fs_ref, ahead_ref, ftab_ref, back_ref,
     out_ref,
     held, acc, wbuf, ss, sm, p0, p1, spec, z_ref, oc_ref,
-    in_own, in_sum, in_low, in_up, in_pad, turned, lower, upper, red_dp, red_z, final,
+    in_own, in_sum, in_low, in_up, in_full, in_pad, turned, lower, upper, red_dp, red_z, final,
     xs, ws, ls, send_l, send_r, recv, psend, precv,
     in_send, low_recv, halo_send, halo_recv,
     dp_send, dp_recv, z_send, z_recv, fin_send, fin_recv,
@@ -116,11 +116,16 @@
             gated = (ss[:, cols].astype(jnp.float32) * sm[:, cols].astype(jnp.float32)).astype(jnp.bfloat16)
             in_sum[...] += lax.dot_general(pi_ref[:, cols], gated, NT, preferred_element_type=jnp.float32)
 
-    def low_copy(peer):
+    def chain_copy(way):
         return pltpu.make_async_remote_copy(
-            src_ref=in_own, dst_ref=in_low.at[z], send_sem=in_send.at[peer], recv_sem=low_recv.at[z],
-            device_id={"pipe": 1, "tensor": peer}, device_id_type=MESH,
-        )
+            src_ref=in_own.at[way], dst_ref=in_low.at[way], send_sem=in_send.at[way], recv_sem=low_recv.at[way],
+            device_id={"tensor": z + 1 - 2 * way}, device_id_type=MESH,
+        )
+
+    full_copy = pltpu.make_async_remote_copy(
+        src_ref=in_sum, dst_ref=in_full, send_sem=in_send.at[2], recv_sem=low_recv.at[2],
+        device_id={"pipe": 1}, device_id_type=MESH,
+    )
 
     def arrived(slots, sems, s):
         pltpu.make_async_copy(slots.at[s], slots.at[s], sems.at[s]).wait()
@@ -149,15 +154,9 @@
     )
 
     def collect():
-        in_sum[...] = jnp.zeros_like(in_sum)
-
-        @pl.loop(0, n)
-        def _(s):
-            arrived(in_low, low_recv, s)
-            in_sum[...] += in_low[s].astype(jnp.float32)
-
+        full_copy.wait_recv()
         for m in range(micro):
-            in_pad[m, :, taps:] = in_sum[:, m * seq : (m + 1) * seq]
+            in_pad[m, :, taps:] = in_full[:, m * seq : (m + 1) * seq]
 
         @pl.when(y < dps - 1)
         def _():
@@ -191,22 +190,44 @@
         for copy in saved_copies:
             copy.start()
         pl.semaphore_signal(barrier, inc=1, device_id={"pipe": 1}, device_id_type=MESH)
-        pl.semaphore_wait(barrier, n)
+
+        @pl.when(has_left)
+        def _():
+            pl.semaphore_signal(barrier, inc=1, device_id={"tensor": z - 1}, device_id_type=MESH)
+
+        @pl.when(has_right)
+        def _():
+            pl.semaphore_signal(barrier, inc=1, device_id={"tensor": z + 1}, device_id_type=MESH)
+
+        pl.semaphore_wait(barrier, 1 + jnp.minimum(z, 1) + jnp.minimum(n - 1 - z, 1))
         p0_copy.start()
         for copy in saved_copies:
             copy.wait()
         in_part()
-        in_own[...] = in_sum[...].astype(jnp.bfloat16)
-
-        @pl.loop(0, n)
-        def _(s):
-            low_copy(s).start()
-
+        in_up[...] = in_sum[...]
+        for way, (sends, takes) in enumerate(((has_right, has_left), (has_left, has_right))):
+            @pl.when(jnp.logical_not(takes))
+            def _():
+                in_low[way] = jnp.zeros(in_low.shape[1:], jnp.bfloat16)
+
+            @pl.when(takes)
+            def _():
+                chain_copy(way).wait_recv()
+
+            @pl.when(sends)
+            def _():
+                in_own[way] = (in_up[...] + in_low[way].astype(jnp.float32)).astype(jnp.bfloat16)
+                chain_copy(way).start()
+
+            in_sum[...] += in_low[way].astype(jnp.float32)
+
+        full_copy.start()
         p0_copy.wait_send()
-
-        @pl.loop(0, n)
-        def _(s):
-            low_copy(s).wait_send()
+        full_copy.wait_send()
+        for way, sends in enumerate((has_right, has_left)):
+            @pl.when(sends)
+            def _():
+                chain_copy(way).wait_send()
 
         fin_copy.wait_recv()
         out_ref[...] = final[:, :, :rank]
@@ -217,10 +238,10 @@
             own_copy(r).start()
         p1_copy = pltpu.make_async_copy(po_hbm, p1, ls.at[2])
 
+        pl.semaphore_signal(barrier, inc=1, device_id={"pipe": 0}, device_id_type=MESH)
+
         @pl.loop(0, n)
         def _(s):
-            pl.semaphore_signal(barrier, inc=1, device_id={"pipe": 0, "tensor": s}, device_id_type=MESH)
-
             @pl.when(s != z)
             def _():
                 pl.semaphore_signal(barrier, inc=1, device_id={"tensor": s}, device_id_type=MESH)
@@ -277,17 +298,9 @@
         if n < 3:
             collect()
 
-        @pl.loop(1, n - 1)
-        def _(k):
-            from_left, from_right = z >= k, z + k < n
-
-            @pl.when(k == n - 2)
-            def _():
-                collect()
-
-            @pl.loop(0, parts)
-            def _(r):
-                @pl.when(from_left)
+        def forward(k, blocks):
+            for r in blocks:
+                @pl.when(z >= k)
                 def _():
                     to_right(z - k, r).wait_recv()
 
@@ -295,7 +308,7 @@
                     def _():
                         to_right(z - k, r).start()
 
-                @pl.when(from_right)
+                @pl.when(z + k < n)
                 def _():
                     to_left(z + k, r).wait_recv()
 
@@ -303,13 +316,29 @@
                     def _():
                         to_left(z + k, r).start()
 
-            @pl.when(from_left)
+        early, late = range(parts // 2), range(parts // 2, parts)
+        if n > 2:
+            forward(1, early)
+
+        @pl.loop(1, n - 1)
+        def _(k):
+            forward(k, late)
+
+            @pl.when(z >= k)
             def _():
                 multiply(z - k)
 
-            @pl.when(from_right)
+            @pl.when(k < n - 2)
+            def _():
+                forward(k + 1, early)
+
+            @pl.when(z + k < n)
             def _():
                 multiply(z + k)
+
+            @pl.when(k == n - 2)
+            def _():
+                collect()
 
         is_end = jnp.logical_or(z == 0, z == n - 1)
         farthest = n - 1 - z
@@ -468,9 +497,10 @@
             pltpu.VMEM((4, size // 2, channels), full),
             pltpu.VMEM((size, rank), full),
             pltpu.VMEM((2, parts, BLOCK, rank), full),
-            pltpu.VMEM((rank, rows), low),
+            pltpu.VMEM((2, rank, rows), low),
             pltpu.VMEM((rank, rows), full),
-            pltpu.VMEM((n, rank, rows), low),
+            pltpu.VMEM((2, rank, rows), low),
+            pltpu.VMEM((rank, rows), full),
             pltpu.VMEM((rank, rows), full),
             pltpu.VMEM((micro, rank, taps + seq), full),
             pltpu.VMEM((parts, rank, size), full),
@@ -482,7 +512,7 @@
             dma((parts,)), dma, dma((3,)),
             dma((n, parts)), dma((n, parts)), dma((n, parts)),
             dma, dma,
-            dma((n,)), dma((n,)), dma, dma,
+            dma((3,)), dma((3,)), dma, dma,
             dma((dps,)), dma((dps,)), dma((n,)), dma((n,)), dma, dma,
         ],
         cost_estimate=pl.CostEstimate(

time: 167 us -> 164 us (0.982)
  Pallas kernels: 165 us -> 162 us
    pallas_call x1, Pallas kernels: 165 us -> 162 us  [body(): pl.pallas_call(functools.partial(kernel, n, tile), out_shape=jax.ShapeDty...]
where the time goes in v5:
time: 164 us
  Pallas kernels  162 us (99%)
    pallas_call x1, Pallas kernels, body(): pl.pallas_call(functools.partial(kernel, n, tile), out_shape=jax.ShapeDty...  162 us

profile of v5, /device:TPU:0, one launch (start us, length us, event | category | flops | bytes accessed | tf_op | source)
XLA Modules:
  0.0 163.6 jit_solution(9070426174636780745)
XLA Ops:
  0.0 162.1 %back_pass.1 = f32[2,64,64]{2,1,0:T(8,128)} custom-call(bf16[1024,2048]{1,0:T(8,128)(2,1)} %bitcast.15, bf16[2048,8192]{1,0:T(8,128)(2,1)} %bitcast.14, bf16[1024,2048]{1,0:T(8,128)(2,1)} %bitcast.16, bf16[1024,2048]{1,0:T(8,128)(2,1)} %bitcast.17, bf16[64,8192]{1,0:T(8,128)(2,1)} %bitcast.18, bf16[64,2048]{1,0:T(8,128)(2,1)} %bitcast.20, ...), custom_call_target="tpu_custom_call" | custom-call | flops 34359738368 | bytes 33554432 | tf_op jit(solution)/shard_map/back_pass/pallas_call | solution.py:484
  162.1 1.5 copy.13

commit v6 on v5

--- a/solution.py
+++ b/solution.py
@@ -33,10 +33,10 @@
     x_hbm, w_hbm, ss_hbm, sm_hbm, po_hbm, pi_ref, fm_ref, fs_ref, ahead_ref, ftab_ref, back_ref,
     out_ref,
     held, acc, wbuf, ss, sm, p0, p1, spec, z_ref, oc_ref,
-    in_own, in_sum, in_low, in_up, in_full, in_pad, turned, lower, upper, red_dp, red_z, final,
+    in_own, in_sum, in_low, in_up, in_full, in_pad, turned, lower, upper, red_dp, red_z, sums,
     xs, ws, ls, send_l, send_r, recv, psend, precv,
     in_send, low_recv, halo_send, halo_recv,
-    dp_send, dp_recv, z_send, z_recv, fin_send, fin_recv,
+    dp_send, dp_recv, z_send, z_recv,
 ):
     z = lax.axis_index("tensor")
     y = lax.axis_index("dp")
@@ -142,16 +142,18 @@
             device_id={"dp": peer}, device_id_type=MESH,
         )
 
-    def z_copy(peer):
+    def z_copy(peer, pipe):
         return pltpu.make_async_remote_copy(
-            src_ref=red_z.at[z], dst_ref=red_z.at[z], send_sem=z_send.at[peer], recv_sem=z_recv.at[z],
-            device_id={"tensor": peer}, device_id_type=MESH,
-        )
-
-    fin_copy = pltpu.make_async_remote_copy(
-        src_ref=final, dst_ref=final, send_sem=fin_send, recv_sem=fin_recv,
-        device_id={"pipe": 0}, device_id_type=MESH,
-    )
+            src_ref=sums.at[pipe], dst_ref=red_z.at[z], send_sem=z_send.at[pipe, peer], recv_sem=z_recv.at[z],
+            device_id={"pipe": pipe, "tensor": peer}, device_id_type=MESH,
+        )
+
+    def give():
+        total = red_z[0]
+        for s in range(1, n):
+            total += red_z[s]
+        for m in range(micro):
+            out_ref[m] = total[:, m * rank : (m + 1) * rank]
 
     def collect():
         full_copy.wait_recv()
@@ -189,7 +191,9 @@
     def _():
         for copy in saved_copies:
             copy.start()
-        pl.semaphore_signal(barrier, inc=1, device_id={"pipe": 1}, device_id_type=MESH)
+        @pl.loop(0, n)
+        def _(s):
+            pl.semaphore_signal(barrier, inc=1, device_id={"pipe": 1, "tensor": s}, device_id_type=MESH)
 
         @pl.when(has_left)
         def _():
@@ -199,7 +203,7 @@
         def _():
             pl.semaphore_signal(barrier, inc=1, device_id={"tensor": z + 1}, device_id_type=MESH)
 
-        pl.semaphore_wait(barrier, 1 + jnp.minimum(z, 1) + jnp.minimum(n - 1 - z, 1))
+        pl.semaphore_wait(barrier, n + jnp.minimum(z, 1) + jnp.minimum(n - 1 - z, 1))
         p0_copy.start()
         for copy in saved_copies:
             copy.wait()
@@ -229,8 +233,11 @@
             def _():
                 chain_copy(way).wait_send()
 
-        fin_copy.wait_recv()
-        out_ref[...] = final[:, :, :rank]
+        @pl.loop(0, n)
+        def _(s):
+            arrived(red_z, z_recv, s)
+
+        give()
 
     @pl.when(top)
     def _():
@@ -238,10 +245,10 @@
             own_copy(r).start()
         p1_copy = pltpu.make_async_copy(po_hbm, p1, ls.at[2])
 
-        pl.semaphore_signal(barrier, inc=1, device_id={"pipe": 0}, device_id_type=MESH)
-
         @pl.loop(0, n)
         def _(s):
+            pl.semaphore_signal(barrier, inc=1, device_id={"pipe": 0, "tensor": s}, device_id_type=MESH)
+
             @pl.when(s != z)
             def _():
                 pl.semaphore_signal(barrier, inc=1, device_id={"tensor": s}, device_id_type=MESH)
@@ -252,7 +259,7 @@
             def _():
                 pl.semaphore_signal(barrier, inc=1, device_id={"dp": s}, device_id_type=MESH)
 
-        pl.semaphore_wait(barrier, n + dps - 1)
+        pl.semaphore_wait(barrier, 2 * n + dps - 2)
 
         for r in range(parts):
             @pl.when(has_left)
@@ -397,8 +404,8 @@
                 in_up[:, span], oc_ref[1, r], precision=high, preferred_element_type=jnp.float32
             )
 
-        for m in range(micro):
-            red_dp[y, m] = jnp.concatenate([lower[m], upper[m]], axis=1) * scale
+        for i, part in enumerate((lower, upper)):
+            red_dp[y, i] = jnp.concatenate([part[m] for m in range(micro)], axis=1) * scale
 
         @pl.loop(0, dps)
         def _(s):
@@ -415,13 +422,16 @@
         total = red_dp[0]
         for s in range(1, dps):
             total += red_dp[s]
-        red_z[z] = total
+        sums[...] = total
+        red_z[z] = total[1]
 
         @pl.loop(0, n)
         def _(s):
+            z_copy(s, 0).start()
+
             @pl.when(s != z)
             def _():
-                z_copy(s).start()
+                z_copy(s, 1).start()
 
         @pl.loop(0, n)
         def _(s):
@@ -429,13 +439,7 @@
             def _():
                 arrived(red_z, z_recv, s)
 
-        total = red_z[0]
-        for s in range(1, n):
-            total += red_z[s]
-        final[...] = total
-        fin_copy.start()
-        out_ref[...] = final[:, :, rank:]
-        fin_copy.wait_send()
+        give()
 
         @pl.when(y < dps - 1)
         def _():
@@ -449,9 +453,11 @@
 
         @pl.loop(0, n)
         def _(s):
+            z_copy(s, 0).wait_send()
+
             @pl.when(s != z)
             def _():
-                z_copy(s).wait_send()
+                z_copy(s, 1).wait_send()
 
             @pl.loop(0, parts)
             def _(r):
@@ -506,14 +512,14 @@
             pltpu.VMEM((parts, rank, size), full),
             pltpu.VMEM((micro, rank, rank), full),
             pltpu.VMEM((micro, rank, rank), full),
-            pltpu.VMEM((dps, micro, rank, 2 * rank), full),
-            pltpu.VMEM((n, micro, rank, 2 * rank), full),
-            pltpu.VMEM((micro, rank, 2 * rank), full),
+            pltpu.VMEM((dps, 2, rank, micro * rank), full),
+            pltpu.VMEM((n, rank, micro * rank), full),
+            pltpu.VMEM((2, rank, micro * rank), full),
             dma((parts,)), dma, dma((3,)),
             dma((n, parts)), dma((n, parts)), dma((n, parts)),
             dma, dma,
             dma((3,)), dma((3,)), dma, dma,
-            dma((dps,)), dma((dps,)), dma((n,)), dma((n,)), dma, dma,
+            dma((dps,)), dma((dps,)), dma((2, n)), dma((n,)),
         ],
         cost_estimate=pl.CostEstimate(
             flops=2 * rows * channels * width * n, bytes_accessed=2 * channels * width * n, transcendentals=0

time: 164 us -> 164 us (level)
  no operation moved by 1% of the time
where the time goes in v6:
time: 164 us; the launch traced here: 163 us
  Pallas kernels  162 us (99%)
    pallas_call x1, Pallas kernels, body(): pl.pallas_call(functools.partial(kernel, n, tile), out_shape=jax.ShapeDty...  162 us

profile of v6, /device:TPU:0, one launch (start us, length us, event | category | flops | bytes accessed | tf_op | source)
XLA Modules:
  0.0 163.3 jit_solution(193588392630218944)
XLA Ops:
  0.0 161.9 %back_pass.1 = f32[2,64,64]{2,1,0:T(8,128)} custom-call(bf16[1024,2048]{1,0:T(8,128)(2,1)} %bitcast.15, bf16[2048,8192]{1,0:T(8,128)(2,1)} %bitcast.14, bf16[1024,2048]{1,0:T(8,128)(2,1)} %bitcast.16, bf16[1024,2048]{1,0:T(8,128)(2,1)} %bitcast.17, bf16[64,8192]{1,0:T(8,128)(2,1)} %bitcast.18, bf16[64,2048]{1,0:T(8,128)(2,1)} %bitcast.20, ...), custom_call_target="tpu_custom_call" | custom-call | flops 34359738368 | bytes 33554432 | tf_op jit(solution)/shard_map/back_pass/pallas_call | solution.py:490
  161.9 1.5 copy.13
